TPU v7x, 128 devices: a whole 4x4x4 slice. The times are simulated.
128 devices in a mesh: outer: 8 (over x_hi, y), inner: 16 (over z, x_lo, core).
Axes of the slice: x: 4 (x_hi: 2, x_lo: 2; x = x_hi * 2 + x_lo), y: 4, z: 4, core: 2. Of those that a mesh axis runs over, the one named last changes fastest.
Arguments:
- stem_activity: float32 [262144, 768], P(('outer', 'inner')), may hold values from -6 to 6
- convolution_weight: bfloat16 [2, 3, 768, 768], replicated, may hold values from -0.125 to 0.125
- convolution_bias: float32 [2, 768], replicated, may hold values from -3 to 3
- query_weight: bfloat16 [768, 768], replicated, as said below
- key_weight: bfloat16 [768, 768], replicated, may hold values from -0.21875 to 0.21875
- value_weight: bfloat16 [768, 768], replicated, may hold values from -0.21875 to 0.21875
- output_weight: bfloat16 [768, 768], replicated, may hold values from -0.21875 to 0.21875
Outputs:
- tower: float32 [262144, 768], P(('outer', 'inner'))
- attended: float32 [2048, 768], P(('outer', 'inner'))
Inputs may be any that keep to these rules, and one draw needn't show every extreme that they name: `query_weight`: Real-valued weights of order 768 ** -0.5 or larger.
All inputs are finite; a program needn't handle non-finite values.
Results may differ from a plain program's by a relative error of at most 0.0003.
Values sent between devices are 32-bit elements; how exact they have to be, the bound alone decides.
A program may use at most 128 MiB of HBM per device.

v0:
```python
import jax
import jax.numpy as jnp
from jax import lax
from jax.sharding import PartitionSpec as P

HEAD_DIM = 64
BASE_DILATION = 4096
POOL = 128


def from_behind(block, axis, distance):
    devices = range(lax.axis_size(axis))
    route = [(i - distance, i) for i in devices if i - distance in devices]
    return lax.ppermute(block, axis, route)


def product(left, right):
    return jnp.dot(
        left,
        right.astype(jnp.float32),
        preferred_element_type=jnp.float32,
        precision=lax.Precision.HIGHEST,
    )


def mix_taps(lower, active, upper, weight, bias):
    conv = product(lower, weight[0]) + product(active, weight[1]) + product(upper, weight[2]) + bias
    return conv


def shards(
    stem_activity,
    convolution_weight,
    convolution_bias,
    query_weight,
    key_weight,
    value_weight,
    output_weight,
):
    sequence_rows, chans = stem_activity.shape
    receptive_field = stem_activity
    for index_of_layer in range(convolution_weight.shape[0]):
        shifted_rows = (BASE_DILATION << index_of_layer) // sequence_rows
        active = jax.nn.gelu(receptive_field, approximate=False)
        lower = from_behind(active, ("outer", "inner"), shifted_rows)
        upper = from_behind(active, ("outer", "inner"), -shifted_rows)
        receptive_field = receptive_field + mix_taps(
            lower,
            active,
            upper,
            convolution_weight[index_of_layer],
            convolution_bias[index_of_layer],
        )
    pooled = receptive_field.reshape(sequence_rows // POOL, POOL, chans).mean(axis=1)
    head_count = chans // HEAD_DIM
    queries = product(pooled, query_weight).reshape(-1, head_count, HEAD_DIM)
    keys_all, vals = (
        lax.all_gather(product(pooled, key_weight), "inner", axis=0, tiled=True),
        lax.all_gather(product(pooled, value_weight), "inner", axis=0, tiled=True),
    )
    keys_all = keys_all.reshape(-1, head_count, HEAD_DIM)
    vals = vals.reshape(-1, head_count, HEAD_DIM)
    scores = jnp.einsum(
        "qhe,khe->hqk", queries, keys_all, precision=lax.Precision.HIGHEST
    ) / jnp.float32(HEAD_DIM**0.5)
    probs = jax.nn.softmax(scores, axis=-1)
    mixed = jnp.einsum("hqk,khe->qhe", probs, vals, precision=lax.Precision.HIGHEST).reshape(
        -1, chans
    )
    attended = pooled + product(mixed, output_weight)
    return (receptive_field, attended)


def solution(mesh):
    return jax.shard_map(
        shards,
        mesh=mesh,
        in_specs=(P(("outer", "inner"), None), P(), P(), P(), P(), P(), P()),
        out_specs=(P(("outer", "inner"), None), P(("outer", "inner"), None)),
        check_vma=False,
    )
```

profile of v0, /device:TPU:4, one launch (start us, length us, event | category | flops | bytes accessed | tf_op | source)
XLA Modules:
  0.0 538.7 jit_solution(3362095417990578467)
XLA Ops:
  0.6 0.0 copy-start
  0.6 0.0 copy-start.3
  0.7 0.0 copy-start.2
  0.7 14.6 %fusion.1 = f32[2048,768]{1,0:T(8,128)S(1)} fusion(f32[2048,768]{1,0:T(8,128)} %param.7), kind=kLoop, calls=%fused_computation.3 | loop fusion | flops 100663296 | bytes 12582912 | tf_op jit(solution)/shard_map/mul | solution.py:44
  15.3 3.1 collective-permute-start
  18.4 7.2 %collective-permute-start.1 = (f32[2048,768]{1,0:T(8,128)S(1)}, f32[2048,768]{1,0:T(8,128)S(1)}, u32[]{:S(2)}, u32[]{:S(2)}) collective-permute-start(f32[2048,768]{1,0:T(8,128)S(1)} %fusion.1), channel_id=1, source_target_pairs={{2,0},{3,1},{4,2},{5,3},{6,4},{7,5},{8,6},{9,7},{10,8},{11,9},{12,... | collective-permute-start | bytes 18874376 | tf_op jit(solution)/shard_map/ppermute | solution.py:14
  25.6 0.0 copy-done.3
  25.7 0.0 copy-done.2
  25.7 0.0 slice-start
  25.7 10.1 %fusion.30 = f32[2048,768]{1,0:T(8,128)} fusion(f32[2048,768]{1,0:T(8,128)S(1)} %fusion.1, bf16[2,3,768,768]{3,2,1,0:T(8,128)(2,1)S(1)} %copy-done.2), kind=kOutput, calls=%fused_computation.47 | convolution fusion | flops 14495514624 | bytes 13762560 | tf_op jit(solution)/shard_map/dot_general | solution.py:18
  35.8 0.0 slice-start.1
  35.8 123.5 %collective-permute-done = f32[2048,768]{1,0:T(8,128)} collective-permute-done((f32[2048,768]{1,0:T(8,128)S(1)}, f32[2048,768]{1,0:T(8,128)}, u32[]{:S(2)}, u32[]{:S(2)}) %collective-permute-start) | collective-permute-done | bytes 6291488 | tf_op jit(solution)/shard_map/ppermute | solution.py:14
  159.3 12.0 %fusion.32 = f32[2048,768]{1,0:T(8,128)} fusion(f32[2048,768]{1,0:T(8,128)} %collective-permute-done, bf16[2,3,768,768]{3,2,1,0:T(8,128)(2,1)S(1)} %copy-done.2), kind=kOutput, calls=%fused_computation.49 | convolution fusion | flops 14495514624 | bytes 13762560 | tf_op jit(solution)/shard_map/dot_general | solution.py:18
  171.3 119.3 %collective-permute-done.1 = f32[2048,768]{1,0:T(8,128)S(1)} collective-permute-done((f32[2048,768]{1,0:T(8,128)S(1)}, f32[2048,768]{1,0:T(8,128)S(1)}, u32[]{:S(2)}, u32[]{:S(2)}) %collective-permute-start.1) | collective-permute-done | bytes 6291488 | tf_op jit(solution)/shard_map/ppermute | solution.py:14
  290.6 0.0 copy-start.4
  290.6 2.7 copy-done.4
  293.3 0.0 slice-done
  293.4 0.0 slice-done.1
  293.4 24.9 %fusion.3 = (f32[2048,768]{1,0:T(8,128)}, f32[2048,768]{1,0:T(8,128)S(1)}) fusion(f32[2048,768]{1,0:T(8,128)S(1)} %bitcast.46, f32[768]{0:T(1024)S(1)} %get-tuple-element.3, f32[2048,768]{1,0:T(8,128)} %copy-done.4, bf16[2,3,768,768]{3,2,1,0:T(8,128)(2,1)S(1)} %copy-done.2, f32[2048,768]{1,0:T(8,128)} %fusion.32, f32[2048,768]{1,0:T(8,128)} %fusion.30), kind=kOutput, calls=%fused_computation.5 | convolution fusion | flops 14602469376 | bytes 38932480 | tf_op jit(solution)/shard_map/dot_general | solution.py:18
  318.2 3.8 collective-permute-start.2
  322.0 7.7 %collective-permute-start.3 = (f32[2048,768]{1,0:T(8,128)}, f32[2048,768]{1,0:T(8,128)S(1)}, u32[]{:S(2)}, u32[]{:S(2)}) collective-permute-start(f32[2048,768]{1,0:T(8,128)} %get-tuple-element.4), channel_id=1, source_target_pairs={{4,0},{5,1},{6,2},{7,3},{8,4},{9,5},{10,6},{11,7},{12,8},{13,9},{1... | collective-permute-start | bytes 18874376 | tf_op jit(solution)/shard_map/ppermute | solution.py:14
  329.8 12.1 %fusion.22 = f32[2048,768]{1,0:T(8,128)} fusion(f32[2048,768]{1,0:T(8,128)} %get-tuple-element.4, bf16[2,3,768,768]{3,2,1,0:T(8,128)(2,1)} %param.8), kind=kOutput, calls=%fused_computation.41 | convolution fusion | flops 14495514624 | bytes 13762560 | tf_op jit(solution)/shard_map/dot_general | solution.py:18
  341.9 120.5 %collective-permute-done.2 = f32[2048,768]{1,0:T(8,128)S(1)} collective-permute-done((f32[2048,768]{1,0:T(8,128)}, f32[2048,768]{1,0:T(8,128)S(1)}, u32[]{:S(2)}, u32[]{:S(2)}) %collective-permute-start.2) | collective-permute-done | bytes 6291488 | tf_op jit(solution)/shard_map/ppermute | solution.py:14
  462.4 11.1 %fusion.24 = f32[2048,768]{1,0:T(8,128)} fusion(f32[2048,768]{1,0:T(8,128)S(1)} %collective-permute-done.2, bf16[2,3,768,768]{3,2,1,0:T(8,128)(2,1)} %param.8), kind=kOutput, calls=%fused_computation.43 | convolution fusion | flops 14495514624 | bytes 13762560 | tf_op jit(solution)/shard_map/dot_general | solution.py:18
  473.5 0.0 collective-permute-done.3
  473.5 14.3 %bitcast_reduce_fusion = (f32[16,768]{1,0:T(8,128)S(1)}, f32[2048,768]{1,0:T(8,128)}) fusion(f32[2048,768]{1,0:T(8,128)S(1)} %get-tuple-element.5, f32[768]{0:T(1024)S(1)} %get-tuple-element.2, f32[2048,768]{1,0:T(8,128)S(1)} %collective-permute-done.3, bf16[2,3,768,768]{3,2,1,0:T(8,128)(2,1)} %param.8, f32[2048,768]{1,0:T(8,128)} %fusion.24, ...), kind=kOutput, calls=%fused_computation.6 | convolution fusion | flops 14503366656 | bytes 32689152 | tf_op jit(solution)/shard_map/dot_general | solution.py:18
  487.9 0.0 copy-start.1
  487.9 0.0 copy-done
  487.9 0.6 fusion.49
  488.5 20.8 %all_gather.6 = f32[256,768]{1,0:T(8,128)S(1)} all-gather(f32[16,768]{1,0:T(8,128)S(1)} %fusion.49), channel_id=1, replica_groups=mesh['outer'=8,'inner'=16] {'inner'}, dimensions={0}, use_global_device_ids=true | all-gather | bytes 835584 | tf_op jit(solution)/shard_map/all_gather | solution.py:59
  509.3 0.3 copy.12
  509.5 0.0 copy-done.1
  509.5 1.9 fusion.45
  511.4 20.8 %all_gather.7 = f32[256,768]{1,0:T(8,128)S(1)} all-gather(f32[16,768]{1,0:T(8,128)S(1)} %fusion.45), channel_id=1, replica_groups=mesh['outer'=8,'inner'=16] {'inner'}, dimensions={0}, use_global_device_ids=true | all-gather | bytes 835584 | tf_op jit(solution)/shard_map/all_gather | solution.py:58
  532.2 0.3 copy.13
  532.5 1.9 fusion.47
  534.3 0.1 reshape.35
  534.4 0.6 fusion.57
  535.0 0.2 fusion.41
  535.2 0.8 convolution_bitcast_fusion
  536.1 0.1 reshape.37
  536.2 2.5 convolution_add_fusion
  (3 shorter events, 0.1 us)
Async XLA Ops:
  0.6 487.2 %copy-start = (bf16[768,768]{1,0:T(8,128)(2,1)S(1)}, bf16[768,768]{1,0:T(8,128)(2,1)}, u32[]{:S(2)}) copy-start(bf16[768,768]{1,0:T(8,128)(2,1)} %param.12) | copy-start | bytes 3538948
  0.6 25.0 %copy-start.3 = (f32[2,768]{1,0:T(2,128)S(1)}, f32[2,768]{1,0:T(2,128)}, u32[]{:S(2)}) copy-start(f32[2,768]{1,0:T(2,128)} %param.9) | copy-start | bytes 18436
  0.7 25.0 %copy-start.2 = (bf16[2,3,768,768]{3,2,1,0:T(8,128)(2,1)S(1)}, bf16[2,3,768,768]{3,2,1,0:T(8,128)(2,1)}, u32[]{:S(2)}) copy-start(bf16[2,3,768,768]{3,2,1,0:T(8,128)(2,1)} %param.8) | copy-start | bytes 21233668
  15.3 144.0 %collective-permute-start = (f32[2048,768]{1,0:T(8,128)S(1)}, f32[2048,768]{1,0:T(8,128)}, u32[]{:S(2)}, u32[]{:S(2)}) collective-permute-start(f32[2048,768]{1,0:T(8,128)S(1)} %fusion.1), channel_id=1, source_target_pairs={{0,2},{1,3},{2,4},{3,5},{4,6},{5,7},{6,8},{7,9},{8,10},{9,11},{10,... | collective-permute-start | bytes 18874376 | tf_op jit(solution)/shard_map/ppermute | solution.py:14
  18.4 272.2 %collective-permute-start.1 = (f32[2048,768]{1,0:T(8,128)S(1)}, f32[2048,768]{1,0:T(8,128)S(1)}, u32[]{:S(2)}, u32[]{:S(2)}) collective-permute-start(f32[2048,768]{1,0:T(8,128)S(1)} %fusion.1), channel_id=1, source_target_pairs={{2,0},{3,1},{4,2},{5,3},{6,4},{7,5},{8,6},{9,7},{10,8},{11,9},{12,... | collective-permute-start | bytes 18874376 | tf_op jit(solution)/shard_map/ppermute | solution.py:14
  25.7 267.7 %slice-start = ((s8[6291456]{0:T(1024)(128)(4,1)}), s8[4194304]{0:T(1024)(128)(4,1)S(1)}, s32[]{:S(2)}) async-start(s8[6291456]{0:T(1024)(128)(4,1)} %bitcast.45), calls=%async_computation | async-start | bytes 8388608
  35.8 257.6 %slice-start.1 = ((s8[6291456]{0:T(1024)(128)(4,1)}), s8[2097152]{0:T(1024)(128)(4,1)S(1)}, s32[]{:S(2)}) async-start(s8[6291456]{0:T(1024)(128)(4,1)} %bitcast.45), calls=%async_computation.1 | async-start | bytes 4194304
  290.6 2.7 copy-start.4
  318.2 144.2 %collective-permute-start.2 = (f32[2048,768]{1,0:T(8,128)}, f32[2048,768]{1,0:T(8,128)S(1)}, u32[]{:S(2)}, u32[]{:S(2)}) collective-permute-start(f32[2048,768]{1,0:T(8,128)} %get-tuple-element.4), channel_id=1, source_target_pairs={{0,4},{1,5},{2,6},{3,7},{4,8},{5,9},{6,10},{7,11},{8,12},{9,13},{1... | collective-permute-start | bytes 18874376 | tf_op jit(solution)/shard_map/ppermute | solution.py:14
  322.0 151.5 %collective-permute-start.3 = (f32[2048,768]{1,0:T(8,128)}, f32[2048,768]{1,0:T(8,128)S(1)}, u32[]{:S(2)}, u32[]{:S(2)}) collective-permute-start(f32[2048,768]{1,0:T(8,128)} %get-tuple-element.4), channel_id=1, source_target_pairs={{4,0},{5,1},{6,2},{7,3},{8,4},{9,5},{10,6},{11,7},{12,8},{13,9},{1... | collective-permute-start | bytes 18874376 | tf_op jit(solution)/shard_map/ppermute | solution.py:14
  487.9 21.7 %copy-start.1 = (f32[16,768]{1,0:T(8,128)}, f32[16,768]{1,0:T(8,128)S(1)}, u32[]{:S(2)}) copy-start(f32[16,768]{1,0:T(8,128)S(1)} %get-tuple-element.6) | copy-start | bytes 147460
where the time goes:
time: 540 us; the launch traced here: 539 us
  waiting for transfers between devices  363 us (67%)
  matrix products  92.7 us (17%)
  blocking collectives  41.6 us (8%)
  starting transfers between devices  21.8 us (4%)
  other arithmetic  14.8 us (3%)
    ppermute x4, waiting for transfers between devices, from_behind(): return lax.ppermute(block, axis, route)  363 us
    dot_general x10, matrix products, product(): jnp.dot(left, right.astype(jnp.float32), preferred_element_type=jnp.float...  91.3 us
    ppermute x4, starting transfers between devices, from_behind(): return lax.ppermute(block, axis, route)  21.8 us
    all_gather x1, blocking collectives, shards(): lax.all_gather(product(pooled, value_weight), 'inner', axis=0, tiled=True)  20.8 us
    all_gather x1, blocking collectives, shards(): lax.all_gather(product(pooled, key_weight), 'inner', axis=0, tiled=True)  20.8 us
    mul x1, other arithmetic, shards(): active = jax.nn.gelu(receptive_field, approximate=False)  14.6 us
  transfers between devices with their start and end apart: 4, of which 3 were waited for; matrix products, arithmetic and copies ran while one was open for 8% of the time, Pallas kernels for 0%

commit v1 on v0

v1 whole, which is shorter than its diff:
```python
import jax
import jax.numpy as jnp
from jax import lax
from jax.experimental import pallas as pl
from jax.experimental.pallas import tpu as pltpu
from jax.sharding import PartitionSpec as P

HEAD_DIM = 64
POOL = 128
GROUPS = 8
MEMBERS = 8
HALO = 3
CHUNKS = 8
IN_FLIGHT = 2
HELD = 4
AHEAD = 2
COLUMNS = 256
PAIR = 2 * HEAD_DIM
MESH = pl.DeviceIdType.MESH
F32, BF16 = jnp.float32, jnp.bfloat16


def gelu(x):
    return 0.5 * x * (1.0 + lax.erf(x * (0.5**0.5)))


def dot(left, right):
    return jnp.dot(left, right, preferred_element_type=F32)


def thirds(value):
    high = value.astype(BF16)
    rest = value - high.astype(F32)
    middle = rest.astype(BF16)
    return high, middle, (rest - middle.astype(F32)).astype(BF16)


def widened(value, weight):
    high, middle, low = thirds(value)
    return (dot(low, weight) + dot(middle, weight)) + dot(high, weight)


def swapped(member, outer):
    return member // 2 * 2 + (member + outer // 4) % 2


def tower_kernel(
    stem, weight, bias, query_weight, key_weight, value_weight, output_weight,
    tower, attended,
    rows_in, rows_out, taps, active, second, field, everyone, mixed, heads_weight,
    weight_sem, heads_sem, in_send, in_recv, halo_send, halo_recv, out_send, out_recv,
    pool_send, pool_recv, share_send, share_recv,
):
    outer, inner = lax.axis_index("outer"), lax.axis_index("inner")
    member, core = inner // 2, inner % 2
    chans = stem.shape[1]
    part = stem.shape[0] // MEMBERS
    rows = part // CHUNKS
    mine = swapped(member, outer)
    up, down = (outer + 1) % GROUPS, (outer + GROUPS - 1) % GROUPS
    neighbours = (
        (up, 2 * swapped(mine, up) + core),
        (down, 2 * swapped(mine, down) + core),
    )

    def other(step):
        return (member // 2 + step // 2) % 4 * 2 + (member + step) % 2

    barrier = pltpu.get_barrier_semaphore()

    def greet(device):
        pl.semaphore_signal(barrier, inc=1, device_id=device, device_id_type=MESH)

    for step in range(1, MEMBERS):
        greet((outer, 2 * other(step) + core))
    greet((outer, inner + 1 - 2 * core))
    for neighbour in neighbours:
        greet(neighbour)

    def load_taps(layer, tap, half):
        return pltpu.make_async_copy(
            weight.at[layer, tap],
            taps.at[layer, tap, pl.ds(half * chans, chans)],
            weight_sem.at[layer, tap, half],
        )

    def load_heads(k):
        source = (query_weight, key_weight, value_weight, output_weight)[k]
        return pltpu.make_async_copy(source, heads_weight.at[k], heads_sem.at[k])

    every_tap = [(layer, tap, half) for layer in range(2) for tap in range(3) for half in range(2)]
    for which in every_tap:
        load_taps(*which).start()
    for k in range(4):
        load_heads(k).start()

    pl.semaphore_wait(barrier, MEMBERS + len(neighbours))

    def span(chunk):
        return pl.ds(pl.multiple_of(chunk * rows, rows), rows)

    def piece(index, chunk):
        return pl.ds(pl.multiple_of(index * part + chunk * rows, rows), rows)

    def send_in(chunk, step):
        to = other(step)
        return pltpu.make_async_remote_copy(
            src_ref=stem.at[piece(swapped(to, outer), chunk)],
            dst_ref=rows_in.at[HALO + member, span(chunk)],
            send_sem=in_send.at[chunk, step],
            recv_sem=in_recv.at[chunk, member],
            device_id=(outer, 2 * to + core),
            device_id_type=MESH,
        )

    def keep_in(chunk):
        return pltpu.make_async_copy(
            stem.at[piece(mine, chunk)], rows_in.at[HALO + member, span(chunk)], in_recv.at[chunk, member]
        )

    def arrived(chunk, block):
        there = rows_in.at[HALO + block, span(chunk)]
        return pltpu.make_async_copy(there, there, in_recv.at[chunk, block])

    def send_halo(chunk, side):
        return pltpu.make_async_remote_copy(
            src_ref=rows_in.at[pl.ds(MEMBERS if side == 0 else HALO, HALO), span(chunk)],
            dst_ref=rows_in.at[pl.ds(0 if side == 0 else HALO + MEMBERS, HALO), span(chunk)],
            send_sem=halo_send.at[chunk, side],
            recv_sem=halo_recv.at[chunk, side],
            device_id=neighbours[side],
            device_id_type=MESH,
        )

    def send_out(chunk, step):
        to = other(step)
        return pltpu.make_async_remote_copy(
            src_ref=rows_out.at[to, span(chunk)],
            dst_ref=tower.at[piece(mine, chunk)],
            send_sem=out_send.at[chunk, step],
            recv_sem=out_recv.at[chunk, mine],
            device_id=(outer, 2 * to + core),
            device_id_type=MESH,
        )

    def keep_out(chunk):
        return pltpu.make_async_copy(
            rows_out.at[member, span(chunk)], tower.at[piece(mine, chunk)], out_recv.at[chunk, mine]
        )

    def returned(chunk, index):
        there = tower.at[piece(index, chunk)]
        return pltpu.make_async_copy(there, there, out_recv.at[chunk, index])

    def start_in(chunk):
        keep_in(chunk).start()
        for step in range(1, MEMBERS):
            send_in(chunk, step).start()

    def start_out(chunk):
        keep_out(chunk).start()
        for step in range(1, MEMBERS):
            send_out(chunk, step).start()

    def forward(chunk):
        for block in range(MEMBERS - HALO, MEMBERS):
            arrived(chunk, block).wait()
        send_halo(chunk, 0).start()
        for block in range(HALO):
            arrived(chunk, block).wait()
        send_halo(chunk, 1).start()
        for block in range(HALO, MEMBERS - HALO):
            arrived(chunk, block).wait()

    def split(value, into, first, columns=slice(0, 768)):
        high = value.astype(BF16)
        count, start, stop = value.shape[0], columns.start, columns.stop
        into[first : first + count, start:stop] = high
        into[first : first + count, chans + start : chans + stop] = (value - high.astype(F32)).astype(BF16)

    def inside(block):
        if 0 <= block < MEMBERS:
            return 1.0
        number = outer * MEMBERS + block
        return ((number >= 0) & (number < GROUPS * MEMBERS)).astype(F32)

    def conv(source, layer, spread, blocks, columns):
        total = bias[layer : layer + 1, columns]
        for tap in range(3):
            first = tap * spread * rows
            total = total + dot(source[first : first + blocks * rows, :], taps[layer, tap, :, columns])
        return total

    tiles = [slice(start, start + COLUMNS) for start in range(0, chans, COLUMNS)]

    def compute(chunk):
        for block in range(MEMBERS + 2 * HALO):
            split(gelu(rows_in[block, span(chunk)]) * inside(block - HALO), active, block * rows)
        for columns in tiles:
            result = conv(active, 0, 1, MEMBERS + 4, columns)
            for block in range(MEMBERS + 4):
                at = slice(block * rows, (block + 1) * rows)
                total = rows_in[block + 1, span(chunk), columns] + result[at]
                field[at, columns] = total
                split(gelu(total) * inside(block - 2), second, block * rows, columns)
        for columns in tiles:
            result = conv(second, 1, 2, MEMBERS, columns)
            for block in range(MEMBERS):
                at = slice(block * rows, (block + 1) * rows)
                before = field[(block + 2) * rows : (block + 3) * rows, columns]
                rows_out[block, span(chunk), columns] = before + result[at]

    def shelf(run, whose):
        return pl.multiple_of((run * 2 + whose) * MEMBERS * MEMBERS, MEMBERS)

    def slot(run, of):
        return pl.ds(shelf(run, core) + of * MEMBERS, MEMBERS)

    def send_pool(run, step):
        return pltpu.make_async_remote_copy(
            src_ref=everyone.at[slot(run, member)],
            dst_ref=everyone.at[slot(run, member)],
            send_sem=pool_send.at[run, step],
            recv_sem=pool_recv.at[run, member],
            device_id=(outer, 2 * other(step) + core),
            device_id_type=MESH,
        )

    def share(run):
        half = pl.ds(shelf(run, core), MEMBERS * MEMBERS)
        return pltpu.make_async_remote_copy(
            src_ref=everyone.at[half],
            dst_ref=everyone.at[half],
            send_sem=share_send.at[run],
            recv_sem=share_recv.at[run],
            device_id=(outer, inner + 1 - 2 * core),
            device_id_type=MESH,
        )

    def start_pool(run):
        everyone[slot(run, member), :] = jnp.concatenate(
            [
                jnp.sum(rows_out[block, run * POOL : (run + 1) * POOL], axis=0, keepdims=True) * (1.0 / POOL)
                for block in range(MEMBERS)
            ],
            axis=0,
        )
        for step in range(1, MEMBERS):
            send_pool(run, step).start()

    def start_share(run):
        for step in range(1, MEMBERS):
            there = everyone.at[slot(run, other(step))]
            pltpu.make_async_copy(there, there, pool_recv.at[run, other(step)]).wait()
        share(run).start()

    def finish_share(run):
        there = everyone.at[pl.ds(shelf(run, 1 - core), MEMBERS * MEMBERS)]
        pltpu.make_async_copy(there, there, share_recv.at[run]).wait()

    for chunk in range(IN_FLIGHT):
        start_in(chunk)
    for chunk in range(AHEAD):
        forward(chunk)
        start_in(chunk + IN_FLIGHT)
    for which in every_tap:
        load_taps(*which).wait()

    def step_of(chunk, _):
        @pl.when(chunk + AHEAD < CHUNKS)
        def _():
            forward(chunk + AHEAD)

        @pl.when(chunk + AHEAD + IN_FLIGHT < CHUNKS)
        def _():
            start_in(chunk + AHEAD + IN_FLIGHT)

        for side in range(2):
            send_halo(chunk, side).wait_recv()
        compute(chunk)

        @pl.when(chunk == HELD - 1)
        def _():
            start_pool(0)

        @pl.when(chunk == HELD + 1)
        def _():
            start_share(0)

        @pl.when(chunk == CHUNKS - 1)
        def _():
            start_pool(1)

        @pl.when(chunk == HELD)
        def _():
            start_out(0)

        @pl.when(chunk >= HELD)
        def _():
            start_out(chunk - HELD + 1)

        return 0

    lax.fori_loop(0, CHUNKS, step_of, 0)
    start_share(1)
    start_out(CHUNKS - HELD + 1)
    for k in range(4):
        load_heads(k).wait()
    finish_share(0)
    finish_share(1)
    for chunk in range(CHUNKS - HELD + 2, CHUNKS):
        start_out(chunk)

    count = MEMBERS * (part // POOL)
    runs = part // POOL
    total = 2 * MEMBERS * count
    parts = thirds(everyone[...])
    place = lax.broadcasted_iota(jnp.int32, (count, total), 0)
    wanted = ((place % runs * 2 + core) * MEMBERS + swapped(place // runs, outer)) * MEMBERS + member
    chosen = (lax.broadcasted_iota(jnp.int32, (count, total), 1) == wanted).astype(F32).astype(BF16)
    own = (dot(chosen, parts[2]) + dot(chosen, parts[1])) + dot(chosen, parts[0])
    lanes = lax.broadcasted_iota(jnp.int32, (1, PAIR), 1)

    def two_heads(pair, _):
        columns = pl.ds(pl.multiple_of(pair * PAIR, PAIR), PAIR)
        queries = widened(own, heads_weight[0, :, columns]) * (HEAD_DIM**-0.5)
        keys = widened(everyone[...], heads_weight[1, :, columns])
        vals = widened(everyone[...], heads_weight[2, :, columns])
        both = jnp.zeros((count, PAIR), F32)
        for half in range(2):
            mask = (lanes // HEAD_DIM == half).astype(F32)
            scores = lax.dot_general(
                queries * mask,
                keys,
                (((1,), (1,)), ((), ())),
                precision=lax.Precision.HIGHEST,
                preferred_element_type=F32,
            )
            powers = jnp.exp(scores - jnp.max(scores, axis=1, keepdims=True))
            probs = powers / jnp.sum(powers, axis=1, keepdims=True)
            both = both + mask * jnp.dot(
                probs, vals, precision=lax.Precision.HIGHEST, preferred_element_type=F32
            )
        mixed[:, columns] = both
        return 0

    lax.fori_loop(0, chans // PAIR, two_heads, 0)
    attended[...] = own + widened(mixed[...], heads_weight[3])

    for run in range(runs):
        share(run).wait_send()
        for step in range(1, MEMBERS):
            send_pool(run, step).wait_send()

    def finish(chunk, _):
        for side in range(2):
            send_halo(chunk, side).wait_send()
        for step in range(1, MEMBERS):
            send_in(chunk, step).wait_send()
            send_out(chunk, step).wait_send()
        for index in range(MEMBERS):
            returned(chunk, index).wait()
        return 0

    lax.fori_loop(0, CHUNKS, finish, 0)


def shards(stem_activity, convolution_weight, convolution_bias, query_weight, key_weight, value_weight, output_weight):
    length, chans = stem_activity.shape
    part = length // MEMBERS
    rows = part // CHUNKS
    blocks = MEMBERS + 2 * HALO
    pooled = length // POOL
    dma, vmem = pltpu.SemaphoreType.DMA, pltpu.VMEM
    far, on_core = pl.BlockSpec(memory_space=pltpu.HBM), pl.BlockSpec(memory_space=vmem)
    return pl.pallas_call(
        tower_kernel,
        out_shape=(
            vmem((length, chans), F32),
            jax.ShapeDtypeStruct((pooled, chans), F32),
        ),
        in_specs=[far, far, on_core, far, far, far, far],
        out_specs=(on_core, on_core),
        scratch_shapes=[
            vmem((blocks, part, chans), F32),
            vmem((MEMBERS, part, chans), F32),
            vmem((2, 3, 2 * chans, chans), BF16),
            vmem((blocks * rows, 2 * chans), BF16),
            vmem(((blocks - 2) * rows, 2 * chans), BF16),
            vmem(((blocks - 2) * rows, chans), F32),
            vmem((2 * MEMBERS * pooled, chans), F32),
            vmem((pooled, chans), F32),
            vmem((4, chans, chans), BF16),
            dma((2, 3, 2)),
            dma((4,)),
            dma((CHUNKS, MEMBERS)),
            dma((CHUNKS, MEMBERS)),
            dma((CHUNKS, 2)),
            dma((CHUNKS, 2)),
            dma((CHUNKS, MEMBERS)),
            dma((CHUNKS, MEMBERS)),
            dma((2, MEMBERS)),
            dma((2, MEMBERS)),
            dma((2,)),
            dma((2,)),
        ],
        compiler_params=pltpu.CompilerParams(
            collective_id=0, has_side_effects=True, vmem_limit_bytes=50 * 1024 * 1024
        ),
        cost_estimate=pl.CostEstimate(
            flops=5 * 2 * 2 * 3 * length * chans * chans, bytes_accessed=8 * length * chans, transcendentals=0
        ),
        name="tower",
    )(
        stem_activity, convolution_weight, convolution_bias,
        query_weight, key_weight, value_weight, output_weight,
    )


def solution(mesh):
    return jax.shard_map(
        shards,
        mesh=mesh,
        in_specs=(P(("outer", "inner"), None), P(), P(), P(), P(), P(), P()),
        out_specs=(P(("outer", "inner"), None), P(("outer", "inner"), None)),
        check_vma=False,
    )
```

time: 540 us -> 158 us (0.29)
  waiting for transfers between devices: 363 us -> 0 us
  Pallas kernels: 0 us -> 151 us
  matrix products: 92.7 us -> 0 us
  blocking collectives: 41.6 us -> 0 us
  starting transfers between devices: 21.8 us -> 0 us
  other arithmetic: 14.8 us -> 0 us
    ppermute x4 -> x0, waiting for transfers between devices: 363 us -> none  [from_behind(): return lax.ppermute(block, axis, route)]
    pallas_call x0 -> x1, Pallas kernels: none -> 151 us  [shards(): pl.pallas_call(tower_kernel, out_shape=(vmem((length, chans), F32), jax.S...]
    dot_general x12 -> x0, matrix products: 92.7 us -> none  [the longest x10 91.3 us: product(): jnp.dot(left, right.astype(jnp.float32), preferred_element_type=jnp.float...]
    all_gather x2 -> x0, blocking collectives: 41.6 us -> none  [the longest x1 20.8 us: shards(): lax.all_gather(product(pooled, value_weight), 'inner', axis=0, tiled=True)]
    ppermute x4 -> x0, starting transfers between devices: 21.8 us -> none  [from_behind(): return lax.ppermute(block, axis, route)]
    mul x1 -> x0, other arithmetic: 14.6 us -> none  [shards(): active = jax.nn.gelu(receptive_field, approximate=False)]
  transfers between devices with their start and end apart: 4 -> 0, of which waited for: 3 -> 0; matrix products, arithmetic and copies ran while one was open for 8% -> 0% of each run, Pallas kernels for 0% -> 0%
where the time goes in v1:
time: 158 us; the launch traced here: 155 us
  Pallas kernels  151 us (96%)
  local copies, waits for them, and re-layouts  3.33 us (2%)
    pallas_call x1, Pallas kernels, shards(): pl.pallas_call(tower_kernel, out_shape=(vmem((length, chans), F32), jax.S...  151 us
    unnamed x4, local copies, waits for them, and re-layouts  3.33 us

profile of v1, /device:TPU:4, one launch (start us, length us, event | category | flops | bytes accessed | tf_op | source)
XLA Modules:
  0.0 155.1 jit_solution(10356464534259957759)
XLA Ops:
  0.6 151.1 %tower.1 = (f32[2048,768]{1,0:T(8,128)S(1)}, f32[16,768]{1,0:T(8,128)}) custom-call(f32[2048,768]{1,0:T(8,128)} %stem.1, bf16[2,3,768,768]{3,2,1,0:T(8,128)(2,1)} %weight.1, f32[2,768]{1,0:T(2,128)} %bias.1, bf16[768,768]{1,0:T(8,128)(2,1)} %query_weight.1, bf16[768,768]{1,0:T(8,128)(2,1)} %key_weight.1, bf16[768,768]{1,0:T(8,128)(2,1)} %value_weight.1, ...), custom_call_target="tpu_custom_call" | custom-call | flops 72477573120 | bytes 12582912 | tf_op jit(solution)/shard_map/tower/pallas_call | solution.py:376
  151.8 0.0 copy-start
  151.8 2.7 %copy.11 = f32[2048,768]{1,0:T(8,128)} copy(f32[2048,768]{1,0:T(8,128)S(1)} %get-tuple-element.2) | data formatting | bytes 12582912
  154.5 0.0 copy-done
  154.5 0.6 copy.12
Async XLA Ops:
  151.8 2.7 %copy-start = (f32[16,768]{1,0:T(8,128)S(1)}, f32[16,768]{1,0:T(8,128)}, u32[]{:S(2)}) copy-start(f32[16,768]{1,0:T(8,128)} %get-tuple-element.7) | copy-start | bytes 147460

commit v2 on v1

--- a/solution.py
+++ b/solution.py
@@ -11,8 +11,8 @@
 MEMBERS = 8
 HALO = 3
 CHUNKS = 8
-IN_FLIGHT = 2
-HELD = 4
+IN_FLIGHT = 3
+HELD = 2
 AHEAD = 2
 COLUMNS = 256
 PAIR = 2 * HEAD_DIM
@@ -279,11 +279,11 @@
             send_halo(chunk, side).wait_recv()
         compute(chunk)
 
-        @pl.when(chunk == HELD - 1)
+        @pl.when(chunk == CHUNKS // 2 - 1)
         def _():
             start_pool(0)
 
-        @pl.when(chunk == HELD + 1)
+        @pl.when(chunk == CHUNKS // 2 + 1)
         def _():
             start_share(0)
 
@@ -291,26 +291,20 @@
         def _():
             start_pool(1)
 
-        @pl.when(chunk == HELD)
-        def _():
-            start_out(0)
-
         @pl.when(chunk >= HELD)
         def _():
-            start_out(chunk - HELD + 1)
+            start_out(chunk - HELD)
 
         return 0
 
     lax.fori_loop(0, CHUNKS, step_of, 0)
     start_share(1)
-    start_out(CHUNKS - HELD + 1)
+    for chunk in range(CHUNKS - HELD, CHUNKS):
+        start_out(chunk)
     for k in range(4):
         load_heads(k).wait()
     finish_share(0)
     finish_share(1)
-    for chunk in range(CHUNKS - HELD + 2, CHUNKS):
-        start_out(chunk)
-
     count = MEMBERS * (part // POOL)
     runs = part // POOL
     total = 2 * MEMBERS * count

time: 158 us -> 158 us (level)
  no operation moved by 1% of the time
where the time goes in v2:
time: 158 us; the launch traced here: 155 us
  Pallas kernels  151 us (96%)
  local copies, waits for them, and re-layouts  3.33 us (2%)
    pallas_call x1, Pallas kernels, shards(): pl.pallas_call(tower_kernel, out_shape=(vmem((length, chans), F32), jax.S...  151 us
    unnamed x4, local copies, waits for them, and re-layouts  3.33 us

profile of v2, /device:TPU:4, one launch (start us, length us, event | category | flops | bytes accessed | tf_op | source)
XLA Modules:
  0.0 155.1 jit_solution(5758887475231392385)
XLA Ops:
  0.6 151.1 %tower.1 = (f32[2048,768]{1,0:T(8,128)S(1)}, f32[16,768]{1,0:T(8,128)}) custom-call(f32[2048,768]{1,0:T(8,128)} %stem.1, bf16[2,3,768,768]{3,2,1,0:T(8,128)(2,1)} %weight.1, f32[2,768]{1,0:T(2,128)} %bias.1, bf16[768,768]{1,0:T(8,128)(2,1)} %query_weight.1, bf16[768,768]{1,0:T(8,128)(2,1)} %key_weight.1, bf16[768,768]{1,0:T(8,128)(2,1)} %value_weight.1, ...), custom_call_target="tpu_custom_call" | custom-call | flops 72477573120 | bytes 12582912 | tf_op jit(solution)/shard_map/tower/pallas_call | solution.py:370
  151.8 0.0 copy-start
  151.8 2.7 %copy.11 = f32[2048,768]{1,0:T(8,128)} copy(f32[2048,768]{1,0:T(8,128)S(1)} %get-tuple-element.2) | data formatting | bytes 12582912
  154.5 0.0 copy-done
  154.5 0.6 copy.12
Async XLA Ops:
  151.8 2.7 %copy-start = (f32[16,768]{1,0:T(8,128)S(1)}, f32[16,768]{1,0:T(8,128)}, u32[]{:S(2)}) copy-start(f32[16,768]{1,0:T(8,128)} %get-tuple-element.7) | copy-start | bytes 147460

commit v3 on v2

--- a/solution.py
+++ b/solution.py
@@ -13,9 +13,9 @@
 CHUNKS = 8
 IN_FLIGHT = 3
 HELD = 2
-AHEAD = 2
+AHEAD = 1
 COLUMNS = 256
-PAIR = 2 * HEAD_DIM
+HEADS_AT_ONCE = 4
 MESH = pl.DeviceIdType.MESH
 F32, BF16 = jnp.float32, jnp.bfloat16
 
@@ -35,11 +35,6 @@
     return high, middle, (rest - middle.astype(F32)).astype(BF16)
 
 
-def widened(value, weight):
-    high, middle, low = thirds(value)
-    return (dot(low, weight) + dot(middle, weight)) + dot(high, weight)
-
-
 def swapped(member, outer):
     return member // 2 * 2 + (member + outer // 4) % 2
 
@@ -47,7 +42,7 @@
 def tower_kernel(
     stem, weight, bias, query_weight, key_weight, value_weight, output_weight,
     tower, attended,
-    rows_in, rows_out, taps, active, second, field, everyone, mixed, heads_weight,
+    rows_in, rows_out, taps, active, second, field, everyone, split_rows, mixed, heads_weight,
     weight_sem, heads_sem, in_send, in_recv, halo_send, halo_recv, out_send, out_recv,
     pool_send, pool_recv, share_send, share_recv,
 ):
@@ -193,9 +188,11 @@
 
     tiles = [slice(start, start + COLUMNS) for start in range(0, chans, COLUMNS)]
 
-    def compute(chunk):
-        for block in range(MEMBERS + 2 * HALO):
+    def activate(chunk, blocks):
+        for block in blocks:
             split(gelu(rows_in[block, span(chunk)]) * inside(block - HALO), active, block * rows)
+
+    def first_layer(chunk):
         for columns in tiles:
             result = conv(active, 0, 1, MEMBERS + 4, columns)
             for block in range(MEMBERS + 4):
@@ -203,12 +200,12 @@
                 total = rows_in[block + 1, span(chunk), columns] + result[at]
                 field[at, columns] = total
                 split(gelu(total) * inside(block - 2), second, block * rows, columns)
-        for columns in tiles:
-            result = conv(second, 1, 2, MEMBERS, columns)
-            for block in range(MEMBERS):
-                at = slice(block * rows, (block + 1) * rows)
-                before = field[(block + 2) * rows : (block + 3) * rows, columns]
-                rows_out[block, span(chunk), columns] = before + result[at]
+
+    def second_layer(chunk, columns):
+        result = conv(second, 1, 2, MEMBERS, columns)
+        for block in range(MEMBERS):
+            before = field[(block + 2) * rows : (block + 3) * rows, columns]
+            rows_out[block, span(chunk), columns] = before + result[block * rows : (block + 1) * rows]
 
     def shelf(run, whose):
         return pl.multiple_of((run * 2 + whose) * MEMBERS * MEMBERS, MEMBERS)
@@ -258,46 +255,56 @@
         there = everyone.at[pl.ds(shelf(run, 1 - core), MEMBERS * MEMBERS)]
         pltpu.make_async_copy(there, there, share_recv.at[run]).wait()
 
+    def bring(chunk):
+        @pl.when(chunk + AHEAD < CHUNKS)
+        def _():
+            forward(chunk + AHEAD)
+
+        @pl.when(chunk + AHEAD + IN_FLIGHT < CHUNKS)
+        def _():
+            start_in(chunk + AHEAD + IN_FLIGHT)
+
+        for side in range(2):
+            send_halo(chunk, side).wait_recv()
+
+    blocks = range(MEMBERS + 2 * HALO)
     for chunk in range(IN_FLIGHT):
         start_in(chunk)
     for chunk in range(AHEAD):
         forward(chunk)
         start_in(chunk + IN_FLIGHT)
+    bring(0)
+    activate(0, blocks)
     for which in every_tap:
         load_taps(*which).wait()
+    first_layer(0)
 
     def step_of(chunk, _):
-        @pl.when(chunk + AHEAD < CHUNKS)
+        bring(chunk)
+        for k, columns in enumerate(tiles):
+            second_layer(chunk - 1, columns)
+            activate(chunk, blocks[k :: len(tiles)])
+        first_layer(chunk)
+
+        @pl.when(chunk > HELD)
         def _():
-            forward(chunk + AHEAD)
-
-        @pl.when(chunk + AHEAD + IN_FLIGHT < CHUNKS)
-        def _():
-            start_in(chunk + AHEAD + IN_FLIGHT)
-
-        for side in range(2):
-            send_halo(chunk, side).wait_recv()
-        compute(chunk)
-
-        @pl.when(chunk == CHUNKS // 2 - 1)
+            start_out(chunk - 1 - HELD)
+
+        @pl.when(chunk == CHUNKS // 2)
         def _():
             start_pool(0)
 
-        @pl.when(chunk == CHUNKS // 2 + 1)
+        @pl.when(chunk == CHUNKS // 2 + 2)
         def _():
             start_share(0)
 
-        @pl.when(chunk == CHUNKS - 1)
-        def _():
-            start_pool(1)
-
-        @pl.when(chunk >= HELD)
-        def _():
-            start_out(chunk - HELD)
-
         return 0
 
-    lax.fori_loop(0, CHUNKS, step_of, 0)
+    lax.fori_loop(1, CHUNKS, step_of, 0)
+    for columns in tiles:
+        second_layer(CHUNKS - 1, columns)
+    start_pool(1)
+    start_out(CHUNKS - 1 - HELD)
     start_share(1)
     for chunk in range(CHUNKS - HELD, CHUNKS):
         start_out(chunk)
@@ -305,41 +312,46 @@
         load_heads(k).wait()
     finish_share(0)
     finish_share(1)
-    count = MEMBERS * (part // POOL)
+
     runs = part // POOL
+    count = MEMBERS * runs
     total = 2 * MEMBERS * count
-    parts = thirds(everyone[...])
+    for k, third in enumerate(thirds(everyone[...])):
+        split_rows[k * total : (k + 1) * total, :] = third
+
+    def stacked(value, weight):
+        size = value.shape[0] // 3
+        result = dot(value, weight)
+        return (result[2 * size :] + result[size : 2 * size]) + result[:size]
+
     place = lax.broadcasted_iota(jnp.int32, (count, total), 0)
     wanted = ((place % runs * 2 + core) * MEMBERS + swapped(place // runs, outer)) * MEMBERS + member
     chosen = (lax.broadcasted_iota(jnp.int32, (count, total), 1) == wanted).astype(F32).astype(BF16)
-    own = (dot(chosen, parts[2]) + dot(chosen, parts[1])) + dot(chosen, parts[0])
-    lanes = lax.broadcasted_iota(jnp.int32, (1, PAIR), 1)
-
-    def two_heads(pair, _):
-        columns = pl.ds(pl.multiple_of(pair * PAIR, PAIR), PAIR)
-        queries = widened(own, heads_weight[0, :, columns]) * (HEAD_DIM**-0.5)
-        keys = widened(everyone[...], heads_weight[1, :, columns])
-        vals = widened(everyone[...], heads_weight[2, :, columns])
-        both = jnp.zeros((count, PAIR), F32)
-        for half in range(2):
-            mask = (lanes // HEAD_DIM == half).astype(F32)
-            scores = lax.dot_general(
-                queries * mask,
-                keys,
-                (((1,), (1,)), ((), ())),
-                precision=lax.Precision.HIGHEST,
-                preferred_element_type=F32,
-            )
-            powers = jnp.exp(scores - jnp.max(scores, axis=1, keepdims=True))
-            probs = powers / jnp.sum(powers, axis=1, keepdims=True)
-            both = both + mask * jnp.dot(
-                probs, vals, precision=lax.Precision.HIGHEST, preferred_element_type=F32
-            )
-        mixed[:, columns] = both
-        return 0
-
-    lax.fori_loop(0, chans // PAIR, two_heads, 0)
-    attended[...] = own + widened(mixed[...], heads_weight[3])
+    own_parts = [dot(chosen, split_rows[k * total : (k + 1) * total, :]) for k in range(3)]
+    own = (own_parts[2] + own_parts[1]) + own_parts[0]
+    own_rows = jnp.concatenate([value.astype(BF16) for value in own_parts], axis=0)
+    width = HEADS_AT_ONCE * HEAD_DIM
+    head = lax.broadcasted_iota(jnp.int32, (1, width), 1) // HEAD_DIM
+    masks = [(head == k).astype(F32) for k in range(HEADS_AT_ONCE)]
+
+    for start in range(0, chans, width):
+        columns = slice(start, start + width)
+        queries = stacked(own_rows, heads_weight[0, :, columns]) * (HEAD_DIM**-0.5)
+        keys = stacked(split_rows[...], heads_weight[1, :, columns])
+        vals = stacked(split_rows[...], heads_weight[2, :, columns])
+        scores = lax.dot_general(
+            jnp.concatenate([queries * mask for mask in masks], axis=0),
+            keys,
+            (((1,), (1,)), ((), ())),
+            precision=lax.Precision.HIGHEST,
+            preferred_element_type=F32,
+        )
+        powers = jnp.exp(scores - jnp.max(scores, axis=1, keepdims=True))
+        probs = powers / jnp.sum(powers, axis=1, keepdims=True)
+        each = jnp.dot(probs, vals, precision=lax.Precision.HIGHEST, preferred_element_type=F32)
+        mixed[:, columns] = sum(each[k * count : (k + 1) * count] * mask for k, mask in enumerate(masks))
+
+    attended[...] = own + stacked(jnp.concatenate(thirds(mixed[...]), axis=0), heads_weight[3])
 
     for run in range(runs):
         share(run).wait_send()
@@ -383,6 +395,7 @@
             vmem(((blocks - 2) * rows, 2 * chans), BF16),
             vmem(((blocks - 2) * rows, chans), F32),
             vmem((2 * MEMBERS * pooled, chans), F32),
+            vmem((3 * 2 * MEMBERS * pooled, chans), BF16),
             vmem((pooled, chans), F32),
             vmem((4, chans, chans), BF16),
             dma((2, 3, 2)),

time: 158 us -> 158 us (level)
  no operation moved by 1% of the time
where the time goes in v3:
time: 158 us; the launch traced here: 155 us
  Pallas kernels  151 us (96%)
  local copies, waits for them, and re-layouts  3.33 us (2%)
    pallas_call x1, Pallas kernels, shards(): pl.pallas_call(tower_kernel, out_shape=(vmem((length, chans), F32), jax.S...  151 us
    unnamed x4, local copies, waits for them, and re-layouts  3.33 us

profile of v3, /device:TPU:4, one launch (start us, length us, event | category | flops | bytes accessed | tf_op | source)
XLA Modules:
  0.0 155.1 jit_solution(12108622384349212441)
XLA Ops:
  0.6 151.1 %tower.1 = (f32[2048,768]{1,0:T(8,128)S(1)}, f32[16,768]{1,0:T(8,128)}) custom-call(f32[2048,768]{1,0:T(8,128)} %stem.1, bf16[2,3,768,768]{3,2,1,0:T(8,128)(2,1)} %weight.1, f32[2,768]{1,0:T(2,128)} %bias.1, bf16[768,768]{1,0:T(8,128)(2,1)} %query_weight.1, bf16[768,768]{1,0:T(8,128)(2,1)} %key_weight.1, bf16[768,768]{1,0:T(8,128)(2,1)} %value_weight.1, ...), custom_call_target="tpu_custom_call" | custom-call | flops 72477573120 | bytes 12582912 | tf_op jit(solution)/shard_map/tower/pallas_call | solution.py:382
  151.8 0.0 copy-start
  151.8 2.7 %copy.11 = f32[2048,768]{1,0:T(8,128)} copy(f32[2048,768]{1,0:T(8,128)S(1)} %get-tuple-element.2) | data formatting | bytes 12582912
  154.5 0.0 copy-done
  154.5 0.6 copy.12
Async XLA Ops:
  151.8 2.7 %copy-start = (f32[16,768]{1,0:T(8,128)S(1)}, f32[16,768]{1,0:T(8,128)}, u32[]{:S(2)}) copy-start(f32[16,768]{1,0:T(8,128)} %get-tuple-element.7) | copy-start | bytes 147460

commit v4 on v3

--- a/solution.py
+++ b/solution.py
@@ -15,6 +15,7 @@
 HELD = 2
 AHEAD = 1
 COLUMNS = 256
+ORDER = (1, 2, 6, 5, 4, 3, 7)
 HEADS_AT_ONCE = 4
 MESH = pl.DeviceIdType.MESH
 F32, BF16 = jnp.float32, jnp.bfloat16
@@ -59,7 +60,8 @@
     )
 
     def other(step):
-        return (member // 2 + step // 2) % 4 * 2 + (member + step) % 2
+        way = step // 2
+        return (member // 2 + way + core * (4 - 2 * way)) % 4 * 2 + (member + step) % 2
 
     barrier = pltpu.get_barrier_semaphore()
 
@@ -149,12 +151,12 @@
 
     def start_in(chunk):
         keep_in(chunk).start()
-        for step in range(1, MEMBERS):
+        for step in ORDER:
             send_in(chunk, step).start()
 
     def start_out(chunk):
         keep_out(chunk).start()
-        for step in range(1, MEMBERS):
+        for step in ORDER:
             send_out(chunk, step).start()
 
     def forward(chunk):

time: 158 us -> 158 us (level)
  no operation moved by 1% of the time
where the time goes in v4:
time: 158 us; the launch traced here: 155 us
  Pallas kernels  151 us (96%)
  local copies, waits for them, and re-layouts  3.33 us (2%)
    pallas_call x1, Pallas kernels, shards(): pl.pallas_call(tower_kernel, out_shape=(vmem((length, chans), F32), jax.S...  151 us
    unnamed x4, local copies, waits for them, and re-layouts  3.33 us

profile of v4, /device:TPU:4, one launch (start us, length us, event | category | flops | bytes accessed | tf_op | source)
XLA Modules:
  0.0 155.1 jit_solution(6925988352330708239)
XLA Ops:
  0.6 151.1 %tower.1 = (f32[2048,768]{1,0:T(8,128)S(1)}, f32[16,768]{1,0:T(8,128)}) custom-call(f32[2048,768]{1,0:T(8,128)} %stem.1, bf16[2,3,768,768]{3,2,1,0:T(8,128)(2,1)} %weight.1, f32[2,768]{1,0:T(2,128)} %bias.1, bf16[768,768]{1,0:T(8,128)(2,1)} %query_weight.1, bf16[768,768]{1,0:T(8,128)(2,1)} %key_weight.1, bf16[768,768]{1,0:T(8,128)(2,1)} %value_weight.1, ...), custom_call_target="tpu_custom_call" | custom-call | flops 72477573120 | bytes 12582912 | tf_op jit(solution)/shard_map/tower/pallas_call | solution.py:384
  151.8 0.0 copy-start
  151.8 2.7 %copy.11 = f32[2048,768]{1,0:T(8,128)} copy(f32[2048,768]{1,0:T(8,128)S(1)} %get-tuple-element.2) | data formatting | bytes 12582912
  154.5 0.0 copy-done
  154.5 0.6 copy.12
Async XLA Ops:
  151.8 2.7 %copy-start = (f32[16,768]{1,0:T(8,128)S(1)}, f32[16,768]{1,0:T(8,128)}, u32[]{:S(2)}) copy-start(f32[16,768]{1,0:T(8,128)} %get-tuple-element.7) | copy-start | bytes 147460

commit v5 on v4

--- a/solution.py
+++ b/solution.py
@@ -16,6 +16,7 @@
 AHEAD = 1
 COLUMNS = 256
 ORDER = (1, 2, 6, 5, 4, 3, 7)
+ROUND = (2, 4, 6)
 HEADS_AT_ONCE = 4
 MESH = pl.DeviceIdType.MESH
 F32, BF16 = jnp.float32, jnp.bfloat16
@@ -215,10 +216,14 @@
     def slot(run, of):
         return pl.ds(shelf(run, core) + of * MEMBERS, MEMBERS)
 
+    def pair(run, of):
+        return pl.ds(shelf(run, core) + of // 2 * 2 * MEMBERS, 2 * MEMBERS)
+
     def send_pool(run, step):
+        part_of = everyone.at[slot(run, member) if step == 1 else pair(run, member)]
         return pltpu.make_async_remote_copy(
-            src_ref=everyone.at[slot(run, member)],
-            dst_ref=everyone.at[slot(run, member)],
+            src_ref=part_of,
+            dst_ref=part_of,
             send_sem=pool_send.at[run, step],
             recv_sem=pool_recv.at[run, member],
             device_id=(outer, 2 * other(step) + core),
@@ -244,12 +249,17 @@
             ],
             axis=0,
         )
-        for step in range(1, MEMBERS):
+        send_pool(run, 1).start()
+
+    def pass_pool(run):
+        there = everyone.at[slot(run, other(1))]
+        pltpu.make_async_copy(there, there, pool_recv.at[run, other(1)]).wait()
+        for step in ROUND:
             send_pool(run, step).start()
 
     def start_share(run):
-        for step in range(1, MEMBERS):
-            there = everyone.at[slot(run, other(step))]
+        for step in ROUND:
+            there = everyone.at[pair(run, other(step))]
             pltpu.make_async_copy(there, there, pool_recv.at[run, other(step)]).wait()
         share(run).start()
 
@@ -296,6 +306,10 @@
         def _():
             start_pool(0)
 
+        @pl.when(chunk == CHUNKS // 2 + 1)
+        def _():
+            pass_pool(0)
+
         @pl.when(chunk == CHUNKS // 2 + 2)
         def _():
             start_share(0)
@@ -307,8 +321,10 @@
         second_layer(CHUNKS - 1, columns)
     start_pool(1)
     start_out(CHUNKS - 1 - HELD)
+    pass_pool(1)
+    start_out(CHUNKS - HELD)
     start_share(1)
-    for chunk in range(CHUNKS - HELD, CHUNKS):
+    for chunk in range(CHUNKS - HELD + 1, CHUNKS):
         start_out(chunk)
     for k in range(4):
         load_heads(k).wait()
@@ -357,7 +373,7 @@
 
     for run in range(runs):
         share(run).wait_send()
-        for step in range(1, MEMBERS):
+        for step in (1, *ROUND):
             send_pool(run, step).wait_send()
 
     def finish(chunk, _):

time: 158 us -> 160 us (1.013)
  Pallas kernels: 151 us -> 154 us
    pallas_call x1, Pallas kernels: 151 us -> 154 us  [shards(): pl.pallas_call(tower_kernel, out_shape=(vmem((length, chans), F32), jax.S...]
where the time goes in v5:
time: 160 us; the launch traced here: 158 us
  Pallas kernels  154 us (96%)
  local copies, waits for them, and re-layouts  3.33 us (2%)
    pallas_call x1, Pallas kernels, shards(): pl.pallas_call(tower_kernel, out_shape=(vmem((length, chans), F32), jax.S...  154 us
    unnamed x4, local copies, waits for them, and re-layouts  3.33 us

profile of v5, /device:TPU:4, one launch (start us, length us, event | category | flops | bytes accessed | tf_op | source)
XLA Modules:
  0.0 158.1 jit_solution(17166375360423186689)
XLA Ops:
  0.6 154.1 %tower.1 = (f32[2048,768]{1,0:T(8,128)S(1)}, f32[16,768]{1,0:T(8,128)}) custom-call(f32[2048,768]{1,0:T(8,128)} %stem.1, bf16[2,3,768,768]{3,2,1,0:T(8,128)(2,1)} %weight.1, f32[2,768]{1,0:T(2,128)} %bias.1, bf16[768,768]{1,0:T(8,128)(2,1)} %query_weight.1, bf16[768,768]{1,0:T(8,128)(2,1)} %key_weight.1, bf16[768,768]{1,0:T(8,128)(2,1)} %value_weight.1, ...), custom_call_target="tpu_custom_call" | custom-call | flops 72477573120 | bytes 12582912 | tf_op jit(solution)/shard_map/tower/pallas_call | solution.py:400
  154.7 0.0 copy-start
  154.7 2.7 %copy.11 = f32[2048,768]{1,0:T(8,128)} copy(f32[2048,768]{1,0:T(8,128)S(1)} %get-tuple-element.2) | data formatting | bytes 12582912
  157.5 0.0 copy-done
  157.5 0.6 copy.12
Async XLA Ops:
  154.7 2.7 %copy-start = (f32[16,768]{1,0:T(8,128)S(1)}, f32[16,768]{1,0:T(8,128)}, u32[]{:S(2)}) copy-start(f32[16,768]{1,0:T(8,128)} %get-tuple-element.7) | copy-start | bytes 147460

commit v6 on v4

--- a/solution.py
+++ b/solution.py
@@ -86,11 +86,6 @@
         return pltpu.make_async_copy(source, heads_weight.at[k], heads_sem.at[k])
 
     every_tap = [(layer, tap, half) for layer in range(2) for tap in range(3) for half in range(2)]
-    for which in every_tap:
-        load_taps(*which).start()
-    for k in range(4):
-        load_heads(k).start()
-
     pl.semaphore_wait(barrier, MEMBERS + len(neighbours))
 
     def span(chunk):
@@ -272,10 +267,14 @@
     blocks = range(MEMBERS + 2 * HALO)
     for chunk in range(IN_FLIGHT):
         start_in(chunk)
+    for which in every_tap:
+        load_taps(*which).start()
     for chunk in range(AHEAD):
         forward(chunk)
         start_in(chunk + IN_FLIGHT)
     bring(0)
+    for k in range(4):
+        load_heads(k).start()
     activate(0, blocks)
     for which in every_tap:
         load_taps(*which).wait()

time: 158 us -> 158 us (level)
  no operation moved by 1% of the time
where the time goes in v6:
time: 158 us; the launch traced here: 155 us
  Pallas kernels  151 us (96%)
  local copies, waits for them, and re-layouts  3.33 us (2%)
    pallas_call x1, Pallas kernels, shards(): pl.pallas_call(tower_kernel, out_shape=(vmem((length, chans), F32), jax.S...  151 us
    unnamed x4, local copies, waits for them, and re-layouts  3.33 us

profile of v6, /device:TPU:4, one launch (start us, length us, event | category | flops | bytes accessed | tf_op | source)
XLA Modules:
  0.0 155.1 jit_solution(11647408518969565032)
XLA Ops:
  0.6 151.1 %tower.1 = (f32[2048,768]{1,0:T(8,128)S(1)}, f32[16,768]{1,0:T(8,128)}) custom-call(f32[2048,768]{1,0:T(8,128)} %stem.1, bf16[2,3,768,768]{3,2,1,0:T(8,128)(2,1)} %weight.1, f32[2,768]{1,0:T(2,128)} %bias.1, bf16[768,768]{1,0:T(8,128)(2,1)} %query_weight.1, bf16[768,768]{1,0:T(8,128)(2,1)} %key_weight.1, bf16[768,768]{1,0:T(8,128)(2,1)} %value_weight.1, ...), custom_call_target="tpu_custom_call" | custom-call | flops 72477573120 | bytes 12582912 | tf_op jit(solution)/shard_map/tower/pallas_call | solution.py:383
  151.8 0.0 copy-start
  151.8 2.7 %copy.11 = f32[2048,768]{1,0:T(8,128)} copy(f32[2048,768]{1,0:T(8,128)S(1)} %get-tuple-element.2) | data formatting | bytes 12582912
  154.5 0.0 copy-done
  154.5 0.6 copy.12
Async XLA Ops:
  151.8 2.7 %copy-start = (f32[16,768]{1,0:T(8,128)S(1)}, f32[16,768]{1,0:T(8,128)}, u32[]{:S(2)}) copy-start(f32[16,768]{1,0:T(8,128)} %get-tuple-element.7) | copy-start | bytes 147460

commit v7 on v6

--- a/solution.py
+++ b/solution.py
@@ -12,10 +12,11 @@
 HALO = 3
 CHUNKS = 8
 IN_FLIGHT = 3
-HELD = 2
+HELD = 4
 AHEAD = 1
 COLUMNS = 256
 ORDER = (1, 2, 6, 5, 4, 3, 7)
+ROUND = (2, 4, 6)
 HEADS_AT_ONCE = 4
 MESH = pl.DeviceIdType.MESH
 F32, BF16 = jnp.float32, jnp.bfloat16
@@ -38,6 +39,10 @@
 
 def swapped(member, outer):
     return member // 2 * 2 + (member + outer // 4) % 2
+
+
+def shelf_place(member):
+    return member % 2 * (MEMBERS // 2) + member // 2
 
 
 def tower_kernel(
@@ -59,6 +64,8 @@
         (down, 2 * swapped(mine, down) + core),
     )
 
+    has = (outer < GROUPS - 1, outer > 0)
+
     def other(step):
         way = step // 2
         return (member // 2 + way + core * (4 - 2 * way)) % 4 * 2 + (member + step) % 2
@@ -71,8 +78,12 @@
     for step in range(1, MEMBERS):
         greet((outer, 2 * other(step) + core))
     greet((outer, inner + 1 - 2 * core))
-    for neighbour in neighbours:
-        greet(neighbour)
+    for neighbour, there in zip(neighbours, has):
+
+        @pl.when(there)
+        def _():
+            greet(neighbour)
+
 
     def load_taps(layer, tap, half):
         return pltpu.make_async_copy(
@@ -86,7 +97,14 @@
         return pltpu.make_async_copy(source, heads_weight.at[k], heads_sem.at[k])
 
     every_tap = [(layer, tap, half) for layer in range(2) for tap in range(3) for half in range(2)]
-    pl.semaphore_wait(barrier, MEMBERS + len(neighbours))
+    for side in range(2):
+        @pl.when(jnp.logical_not(has[side]))
+        def _():
+            rows_in[0 if side else HALO + MEMBERS : HALO if side else 2 * HALO + MEMBERS] = jnp.zeros(
+                (HALO, part, chans), F32
+            )
+
+    pl.semaphore_wait(barrier, MEMBERS + has[0].astype(jnp.int32) + has[1].astype(jnp.int32))
 
     def span(chunk):
         return pl.ds(pl.multiple_of(chunk * rows, rows), rows)
@@ -157,10 +175,18 @@
     def forward(chunk):
         for block in range(MEMBERS - HALO, MEMBERS):
             arrived(chunk, block).wait()
-        send_halo(chunk, 0).start()
+
+        @pl.when(has[0])
+        def _():
+            send_halo(chunk, 0).start()
+
         for block in range(HALO):
             arrived(chunk, block).wait()
-        send_halo(chunk, 1).start()
+
+        @pl.when(has[1])
+        def _():
+            send_halo(chunk, 1).start()
+
         for block in range(HALO, MEMBERS - HALO):
             arrived(chunk, block).wait()
 
@@ -208,12 +234,16 @@
         return pl.multiple_of((run * 2 + whose) * MEMBERS * MEMBERS, MEMBERS)
 
     def slot(run, of):
-        return pl.ds(shelf(run, core) + of * MEMBERS, MEMBERS)
+        return pl.ds(shelf(run, core) + shelf_place(of) * MEMBERS, MEMBERS)
+
+    def column(run, of):
+        return pl.ds(shelf(run, core) + of % 2 * (MEMBERS // 2 * MEMBERS), MEMBERS // 2 * MEMBERS)
 
     def send_pool(run, step):
+        part_of = everyone.at[column(run, member) if step == 1 else slot(run, member)]
         return pltpu.make_async_remote_copy(
-            src_ref=everyone.at[slot(run, member)],
-            dst_ref=everyone.at[slot(run, member)],
+            src_ref=part_of,
+            dst_ref=part_of,
             send_sem=pool_send.at[run, step],
             recv_sem=pool_recv.at[run, member],
             device_id=(outer, 2 * other(step) + core),
@@ -239,13 +269,18 @@
             ],
             axis=0,
         )
-        for step in range(1, MEMBERS):
+        for step in ROUND:
             send_pool(run, step).start()
 
-    def start_share(run):
-        for step in range(1, MEMBERS):
+    def pass_pool(run):
+        for step in ROUND:
             there = everyone.at[slot(run, other(step))]
             pltpu.make_async_copy(there, there, pool_recv.at[run, other(step)]).wait()
+        send_pool(run, 1).start()
+
+    def start_share(run):
+        there = everyone.at[column(run, other(1))]
+        pltpu.make_async_copy(there, there, pool_recv.at[run, other(1)]).wait()
         share(run).start()
 
     def finish_share(run):
@@ -262,7 +297,10 @@
             start_in(chunk + AHEAD + IN_FLIGHT)
 
         for side in range(2):
-            send_halo(chunk, side).wait_recv()
+
+            @pl.when(has[1 - side])
+            def _():
+                send_halo(chunk, side).wait_recv()
 
     blocks = range(MEMBERS + 2 * HALO)
     for chunk in range(IN_FLIGHT):
@@ -287,13 +325,21 @@
             activate(chunk, blocks[k :: len(tiles)])
         first_layer(chunk)
 
-        @pl.when(chunk > HELD)
-        def _():
-            start_out(chunk - 1 - HELD)
+        @pl.when(chunk == HELD)
+        def _():
+            start_out(0)
+
+        @pl.when(chunk >= HELD)
+        def _():
+            start_out(chunk - HELD + 1)
 
         @pl.when(chunk == CHUNKS // 2)
         def _():
             start_pool(0)
+
+        @pl.when(chunk == CHUNKS // 2 + 1)
+        def _():
+            pass_pool(0)
 
         @pl.when(chunk == CHUNKS // 2 + 2)
         def _():
@@ -305,9 +351,11 @@
     for columns in tiles:
         second_layer(CHUNKS - 1, columns)
     start_pool(1)
-    start_out(CHUNKS - 1 - HELD)
+    start_out(CHUNKS - HELD + 1)
+    pass_pool(1)
+    start_out(CHUNKS - HELD + 2)
     start_share(1)
-    for chunk in range(CHUNKS - HELD, CHUNKS):
+    for chunk in range(CHUNKS - HELD + 3, CHUNKS):
         start_out(chunk)
     for k in range(4):
         load_heads(k).wait()
@@ -326,7 +374,7 @@
         return (result[2 * size :] + result[size : 2 * size]) + result[:size]
 
     place = lax.broadcasted_iota(jnp.int32, (count, total), 0)
-    wanted = ((place % runs * 2 + core) * MEMBERS + swapped(place // runs, outer)) * MEMBERS + member
+    wanted = ((place % runs * 2 + core) * MEMBERS + shelf_place(swapped(place // runs, outer))) * MEMBERS + member
     chosen = (lax.broadcasted_iota(jnp.int32, (count, total), 1) == wanted).astype(F32).astype(BF16)
     own_parts = [dot(chosen, split_rows[k * total : (k + 1) * total, :]) for k in range(3)]
     own = (own_parts[2] + own_parts[1]) + own_parts[0]
@@ -356,12 +404,16 @@
 
     for run in range(runs):
         share(run).wait_send()
-        for step in range(1, MEMBERS):
+        for step in (1, *ROUND):
             send_pool(run, step).wait_send()
 
     def finish(chunk, _):
         for side in range(2):
-            send_halo(chunk, side).wait_send()
+
+            @pl.when(has[side])
+            def _():
+                send_halo(chunk, side).wait_send()
+
         for step in range(1, MEMBERS):
             send_in(chunk, step).wait_send()
             send_out(chunk, step).wait_send()

time: 158 us -> 155 us (0.981); the launches traced: 155 us -> 155 us
  no operation moved by 1% of the time
where the time goes in v7:
time: 155 us
  Pallas kernels  151 us (97%)
  local copies, waits for them, and re-layouts  3.33 us (2%)
    pallas_call x1, Pallas kernels, shards(): pl.pallas_call(tower_kernel, out_shape=(vmem((length, chans), F32), jax.S...  151 us
    unnamed x4, local copies, waits for them, and re-layouts  3.33 us

profile of v7, /device:TPU:4, one launch (start us, length us, event | category | flops | bytes accessed | tf_op | source)
XLA Modules:
  0.0 155.2 jit_solution(1780985300239446751)
XLA Ops:
  0.6 151.3 %tower.1 = (f32[2048,768]{1,0:T(8,128)S(1)}, f32[16,768]{1,0:T(8,128)}) custom-call(f32[2048,768]{1,0:T(8,128)} %stem.1, bf16[2,3,768,768]{3,2,1,0:T(8,128)(2,1)} %weight.1, f32[2,768]{1,0:T(2,128)} %bias.1, bf16[768,768]{1,0:T(8,128)(2,1)} %query_weight.1, bf16[768,768]{1,0:T(8,128)(2,1)} %key_weight.1, bf16[768,768]{1,0:T(8,128)(2,1)} %value_weight.1, ...), custom_call_target="tpu_custom_call" | custom-call | flops 72477573120 | bytes 12582912 | tf_op jit(solution)/shard_map/tower/pallas_call | solution.py:435
  151.9 0.0 copy-start
  151.9 2.7 %copy.11 = f32[2048,768]{1,0:T(8,128)} copy(f32[2048,768]{1,0:T(8,128)S(1)} %get-tuple-element.2) | data formatting | bytes 12582912
  154.6 0.0 copy-done
  154.6 0.6 copy.12
Async XLA Ops:
  151.9 2.7 %copy-start = (f32[16,768]{1,0:T(8,128)S(1)}, f32[16,768]{1,0:T(8,128)}, u32[]{:S(2)}) copy-start(f32[16,768]{1,0:T(8,128)} %get-tuple-element.7) | copy-start | bytes 147460

commit v8 on v7

--- a/solution.py
+++ b/solution.py
@@ -10,9 +10,9 @@
 GROUPS = 8
 MEMBERS = 8
 HALO = 3
-CHUNKS = 8
+CHUNKS = 4
 IN_FLIGHT = 3
-HELD = 4
+HELD = 2
 AHEAD = 1
 COLUMNS = 256
 ORDER = (1, 2, 6, 5, 4, 3, 7)
@@ -341,22 +341,16 @@
         def _():
             pass_pool(0)
 
-        @pl.when(chunk == CHUNKS // 2 + 2)
-        def _():
-            start_share(0)
-
         return 0
 
     lax.fori_loop(1, CHUNKS, step_of, 0)
     for columns in tiles:
         second_layer(CHUNKS - 1, columns)
     start_pool(1)
+    start_share(0)
     start_out(CHUNKS - HELD + 1)
     pass_pool(1)
-    start_out(CHUNKS - HELD + 2)
     start_share(1)
-    for chunk in range(CHUNKS - HELD + 3, CHUNKS):
-        start_out(chunk)
     for k in range(4):
         load_heads(k).wait()
     finish_share(0)

time: 155 us -> 175 us (1.13)
  Pallas kernels: 151 us -> 170 us
    pallas_call x1, Pallas kernels: 151 us -> 170 us  [shards(): pl.pallas_call(tower_kernel, out_shape=(vmem((length, chans), F32), jax.S...]
where the time goes in v8:
time: 175 us; the launch traced here: 174 us
  Pallas kernels  170 us (97%)
  local copies, waits for them, and re-layouts  3.33 us (2%)
    pallas_call x1, Pallas kernels, shards(): pl.pallas_call(tower_kernel, out_shape=(vmem((length, chans), F32), jax.S...  170 us

profile of v8, /device:TPU:4, one launch (start us, length us, event | category | flops | bytes accessed | tf_op | source)
XLA Modules:
  0.0 173.7 jit_solution(5181704972406121014)
XLA Ops:
  0.6 169.7 %tower.1 = (f32[2048,768]{1,0:T(8,128)S(1)}, f32[16,768]{1,0:T(8,128)}) custom-call(f32[2048,768]{1,0:T(8,128)} %stem.1, bf16[2,3,768,768]{3,2,1,0:T(8,128)(2,1)} %weight.1, f32[2,768]{1,0:T(2,128)} %bias.1, bf16[768,768]{1,0:T(8,128)(2,1)} %query_weight.1, bf16[768,768]{1,0:T(8,128)(2,1)} %key_weight.1, bf16[768,768]{1,0:T(8,128)(2,1)} %value_weight.1, ...), custom_call_target="tpu_custom_call" | custom-call | flops 72477573120 | bytes 12582912 | tf_op jit(solution)/shard_map/tower/pallas_call | solution.py:429
  170.4 0.0 copy-start
  170.4 2.7 %copy.11 = f32[2048,768]{1,0:T(8,128)} copy(f32[2048,768]{1,0:T(8,128)S(1)} %get-tuple-element.2) | data formatting | bytes 12582912
  173.1 0.0 copy-done
  173.1 0.6 copy.12
Async XLA Ops:
  170.4 2.7 %copy-start = (f32[16,768]{1,0:T(8,128)S(1)}, f32[16,768]{1,0:T(8,128)}, u32[]{:S(2)}) copy-start(f32[16,768]{1,0:T(8,128)} %get-tuple-element.7) | copy-start | bytes 147460

commit v9 on v7

--- a/solution.py
+++ b/solution.py
@@ -239,16 +239,27 @@
     def column(run, of):
         return pl.ds(shelf(run, core) + of % 2 * (MEMBERS // 2 * MEMBERS), MEMBERS // 2 * MEMBERS)
 
-    def send_pool(run, step):
-        part_of = everyone.at[column(run, member) if step == 1 else slot(run, member)]
+    def send_pool(run, lot, step):
+        part_of = everyone.at[(slot(run, member), slot(run, other(1)), column(run, member))[lot]]
         return pltpu.make_async_remote_copy(
             src_ref=part_of,
             dst_ref=part_of,
-            send_sem=pool_send.at[run, step],
-            recv_sem=pool_recv.at[run, member],
+            send_sem=pool_send.at[run, lot, step],
+            recv_sem=pool_recv.at[run, lot, member],
             device_id=(outer, 2 * other(step) + core),
             device_id_type=MESH,
         )
+
+    def pool_arrived(run, lot, step):
+        origin = other(step)
+        across = origin // 2 * 2 + 1 - origin % 2
+        there = everyone.at[(slot(run, origin), slot(run, across), column(run, origin))[lot]]
+        pltpu.make_async_copy(there, there, pool_recv.at[run, lot, origin]).wait()
+
+    pool_legs = (
+        ([(0, 1)], [(lot, step) for lot in (0, 1) for step in ROUND]),
+        ([(0, step) for step in ROUND], [(2, 1)]),
+    )
 
     def share(run):
         half = pl.ds(shelf(run, core), MEMBERS * MEMBERS)
@@ -269,18 +280,18 @@
             ],
             axis=0,
         )
-        for step in ROUND:
-            send_pool(run, step).start()
+        for lot, step in pool_legs[run][0]:
+            send_pool(run, lot, step).start()
 
     def pass_pool(run):
-        for step in ROUND:
-            there = everyone.at[slot(run, other(step))]
-            pltpu.make_async_copy(there, there, pool_recv.at[run, other(step)]).wait()
-        send_pool(run, 1).start()
+        for lot, step in pool_legs[run][0]:
+            pool_arrived(run, lot, step)
+        for lot, step in pool_legs[run][1]:
+            send_pool(run, lot, step).start()
 
     def start_share(run):
-        there = everyone.at[column(run, other(1))]
-        pltpu.make_async_copy(there, there, pool_recv.at[run, other(1)]).wait()
+        for lot, step in pool_legs[run][1]:
+            pool_arrived(run, lot, step)
         share(run).start()
 
     def finish_share(run):
@@ -404,8 +415,8 @@
 
     for run in range(runs):
         share(run).wait_send()
-        for step in (1, *ROUND):
-            send_pool(run, step).wait_send()
+        for lot, step in pool_legs[run][0] + pool_legs[run][1]:
+            send_pool(run, lot, step).wait_send()
 
     def finish(chunk, _):
         for side in range(2):
@@ -459,8 +470,8 @@
             dma((CHUNKS, 2)),
             dma((CHUNKS, MEMBERS)),
             dma((CHUNKS, MEMBERS)),
-            dma((2, MEMBERS)),
-            dma((2, MEMBERS)),
+            dma((2, 3, MEMBERS)),
+            dma((2, 3, MEMBERS)),
             dma((2,)),
             dma((2,)),
         ],

time: 155 us -> 157 us (1.013)
  Pallas kernels: 151 us -> 153 us
where the time goes in v9:
time: 157 us; the launch traced here: 156 us
  Pallas kernels  153 us (97%)
  local copies, waits for them, and re-layouts  3.33 us (2%)
    pallas_call x1, Pallas kernels, shards(): pl.pallas_call(tower_kernel, out_shape=(vmem((length, chans), F32), jax.S...  153 us
    unnamed x4, local copies, waits for them, and re-layouts  3.33 us

profile of v9, /device:TPU:4, one launch (start us, length us, event | category | flops | bytes accessed | tf_op | source)
XLA Modules:
  0.0 156.5 jit_solution(11228531686168130619)
XLA Ops:
  0.6 152.5 %tower.1 = (f32[2048,768]{1,0:T(8,128)S(1)}, f32[16,768]{1,0:T(8,128)}) custom-call(f32[2048,768]{1,0:T(8,128)} %stem.1, bf16[2,3,768,768]{3,2,1,0:T(8,128)(2,1)} %weight.1, f32[2,768]{1,0:T(2,128)} %bias.1, bf16[768,768]{1,0:T(8,128)(2,1)} %query_weight.1, bf16[768,768]{1,0:T(8,128)(2,1)} %key_weight.1, bf16[768,768]{1,0:T(8,128)(2,1)} %value_weight.1, ...), custom_call_target="tpu_custom_call" | custom-call | flops 72477573120 | bytes 12582912 | tf_op jit(solution)/shard_map/tower/pallas_call | solution.py:446
  153.2 0.0 copy-start
  153.2 2.7 %copy.11 = f32[2048,768]{1,0:T(8,128)} copy(f32[2048,768]{1,0:T(8,128)S(1)} %get-tuple-element.2) | data formatting | bytes 12582912
  155.9 0.0 copy-done
  155.9 0.6 copy.12
Async XLA Ops:
  153.2 2.7 %copy-start = (f32[16,768]{1,0:T(8,128)S(1)}, f32[16,768]{1,0:T(8,128)}, u32[]{:S(2)}) copy-start(f32[16,768]{1,0:T(8,128)} %get-tuple-element.7) | copy-start | bytes 147460

commit v10 on v7

--- a/solution.py
+++ b/solution.py
@@ -22,8 +22,43 @@
 F32, BF16 = jnp.float32, jnp.bfloat16
 
 
+EDGE = 4.0 * 2.0**0.5
+NUMERATOR = (
+    -1.60960333262415e-02,
+    -2.95459980854025e-03,
+    -7.34990630326855e-04,
+    -5.69250639462346e-05,
+    -2.10102402082508e-06,
+    2.77068142495902e-08,
+    -2.72614225801306e-10,
+)
+DENOMINATOR = (
+    -1.42647390514189e-02,
+    -7.37332916720468e-03,
+    -1.68282697438203e-03,
+    -2.13374055278905e-04,
+    -1.45660718464996e-05,
+)
+
+
+def horner(square, factors, scale):
+    terms = [factor * scale * 0.5**k for k, factor in enumerate(factors)]
+    total = terms[-1]
+    for term in terms[-2::-1]:
+        total = total * square + term
+    return total
+
+
 def gelu(x):
-    return 0.5 * x * (1.0 + lax.erf(x * (0.5**0.5)))
+    inner = jnp.minimum(jnp.maximum(x, -EDGE), EDGE)
+    square = inner * inner
+    below = horner(square, DENOMINATOR, 1.0)
+    inverse = pl.reciprocal(below, approx=True)
+    inverse = inverse * (2.0 - below * inverse)
+    inverse = inverse * (2.0 - below * inverse)
+    ratio = inner * horner(square, NUMERATOR, 0.5**0.5) * inverse
+    half = 0.5 * x
+    return half + half * jnp.minimum(jnp.maximum(ratio, -1.0), 1.0)
 
 
 def dot(left, right):
@@ -88,7 +123,7 @@
     def load_taps(layer, tap, half):
         return pltpu.make_async_copy(
             weight.at[layer, tap],
-            taps.at[layer, tap, pl.ds(half * chans, chans)],
+            taps.at[layer, pl.ds((2 * tap + half) * chans, chans)],
             weight_sem.at[layer, tap, half],
         )
 
@@ -203,11 +238,9 @@
         return ((number >= 0) & (number < GROUPS * MEMBERS)).astype(F32)
 
     def conv(source, layer, spread, blocks, columns):
-        total = bias[layer : layer + 1, columns]
-        for tap in range(3):
-            first = tap * spread * rows
-            total = total + dot(source[first : first + blocks * rows, :], taps[layer, tap, :, columns])
-        return total
+        lower = [tap * spread * rows for tap in range(3)]
+        shifted = jnp.concatenate([source[first : first + blocks * rows, :] for first in lower], axis=1)
+        return dot(shifted, taps[layer, :, columns]) + bias[layer : layer + 1, columns]
 
     tiles = [slice(start, start + COLUMNS) for start in range(0, chans, COLUMNS)]
 
@@ -443,7 +476,7 @@
         scratch_shapes=[
             vmem((blocks, part, chans), F32),
             vmem((MEMBERS, part, chans), F32),
-            vmem((2, 3, 2 * chans, chans), BF16),
+            vmem((2, 3 * 2 * chans, chans), BF16),
             vmem((blocks * rows, 2 * chans), BF16),
             vmem(((blocks - 2) * rows, 2 * chans), BF16),
             vmem(((blocks - 2) * rows, chans), F32),

time: 155 us -> 156 us (level)
  no operation moved by 1% of the time
where the time goes in v10:
time: 156 us
  Pallas kernels  152 us (97%)
  local copies, waits for them, and re-layouts  3.33 us (2%)
    pallas_call x1, Pallas kernels, shards(): pl.pallas_call(tower_kernel, out_shape=(vmem((length, chans), F32), jax.S...  152 us
    unnamed x4, local copies, waits for them, and re-layouts  3.33 us

profile of v10, /device:TPU:4, one launch (start us, length us, event | category | flops | bytes accessed | tf_op | source)
XLA Modules:
  0.0 155.8 jit_solution(5904629757223234071)
XLA Ops:
  0.6 151.8 %tower.1 = (f32[2048,768]{1,0:T(8,128)S(1)}, f32[16,768]{1,0:T(8,128)}) custom-call(f32[2048,768]{1,0:T(8,128)} %stem.1, bf16[2,3,768,768]{3,2,1,0:T(8,128)(2,1)} %weight.1, f32[2,768]{1,0:T(2,128)} %bias.1, bf16[768,768]{1,0:T(8,128)(2,1)} %query_weight.1, bf16[768,768]{1,0:T(8,128)(2,1)} %key_weight.1, bf16[768,768]{1,0:T(8,128)(2,1)} %value_weight.1, ...), custom_call_target="tpu_custom_call" | custom-call | flops 72477573120 | bytes 12582912 | tf_op jit(solution)/shard_map/tower/pallas_call | solution.py:468
  152.5 0.0 copy-start
  152.5 2.7 %copy.11 = f32[2048,768]{1,0:T(8,128)} copy(f32[2048,768]{1,0:T(8,128)S(1)} %get-tuple-element.2) | data formatting | bytes 12582912
  155.2 0.0 copy-done
  155.2 0.6 copy.12
Async XLA Ops:
  152.5 2.7 %copy-start = (f32[16,768]{1,0:T(8,128)S(1)}, f32[16,768]{1,0:T(8,128)}, u32[]{:S(2)}) copy-start(f32[16,768]{1,0:T(8,128)} %get-tuple-element.7) | copy-start | bytes 147460

commit v11 on v7

--- a/solution.py
+++ b/solution.py
@@ -12,11 +12,10 @@
 HALO = 3
 CHUNKS = 8
 IN_FLIGHT = 3
-HELD = 4
+HELD = 3
 AHEAD = 1
 COLUMNS = 256
 ORDER = (1, 2, 6, 5, 4, 3, 7)
-ROUND = (2, 4, 6)
 HEADS_AT_ONCE = 4
 MESH = pl.DeviceIdType.MESH
 F32, BF16 = jnp.float32, jnp.bfloat16
@@ -236,11 +235,8 @@
     def slot(run, of):
         return pl.ds(shelf(run, core) + shelf_place(of) * MEMBERS, MEMBERS)
 
-    def column(run, of):
-        return pl.ds(shelf(run, core) + of % 2 * (MEMBERS // 2 * MEMBERS), MEMBERS // 2 * MEMBERS)
-
     def send_pool(run, step):
-        part_of = everyone.at[column(run, member) if step == 1 else slot(run, member)]
+        part_of = everyone.at[slot(run, member)]
         return pltpu.make_async_remote_copy(
             src_ref=part_of,
             dst_ref=part_of,
@@ -269,18 +265,13 @@
             ],
             axis=0,
         )
-        for step in ROUND:
+        for step in ORDER:
             send_pool(run, step).start()
 
-    def pass_pool(run):
-        for step in ROUND:
+    def start_share(run):
+        for step in ORDER:
             there = everyone.at[slot(run, other(step))]
             pltpu.make_async_copy(there, there, pool_recv.at[run, other(step)]).wait()
-        send_pool(run, 1).start()
-
-    def start_share(run):
-        there = everyone.at[column(run, other(1))]
-        pltpu.make_async_copy(there, there, pool_recv.at[run, other(1)]).wait()
         share(run).start()
 
     def finish_share(run):
@@ -337,10 +328,6 @@
         def _():
             start_pool(0)
 
-        @pl.when(chunk == CHUNKS // 2 + 1)
-        def _():
-            pass_pool(0)
-
         @pl.when(chunk == CHUNKS // 2 + 2)
         def _():
             start_share(0)
@@ -352,10 +339,8 @@
         second_layer(CHUNKS - 1, columns)
     start_pool(1)
     start_out(CHUNKS - HELD + 1)
-    pass_pool(1)
-    start_out(CHUNKS - HELD + 2)
     start_share(1)
-    for chunk in range(CHUNKS - HELD + 3, CHUNKS):
+    for chunk in range(CHUNKS - HELD + 2, CHUNKS):
         start_out(chunk)
     for k in range(4):
         load_heads(k).wait()
@@ -404,7 +389,7 @@
 
     for run in range(runs):
         share(run).wait_send()
-        for step in (1, *ROUND):
+        for step in ORDER:
             send_pool(run, step).wait_send()
 
     def finish(chunk, _):

time: 155 us -> 155 us (level)
  no operation moved by 1% of the time
where the time goes in v11:
time: 155 us
  Pallas kernels  151 us (97%)
  local copies, waits for them, and re-layouts  3.33 us (2%)
    pallas_call x1, Pallas kernels, shards(): pl.pallas_call(tower_kernel, out_shape=(vmem((length, chans), F32), jax.S...  151 us
    unnamed x4, local copies, waits for them, and re-layouts  3.33 us

profile of v11, /device:TPU:4, one launch (start us, length us, event | category | flops | bytes accessed | tf_op | source)
XLA Modules:
  0.0 155.1 jit_solution(16056730855827311856)
XLA Ops:
  0.6 151.1 %tower.1 = (f32[2048,768]{1,0:T(8,128)S(1)}, f32[16,768]{1,0:T(8,128)}) custom-call(f32[2048,768]{1,0:T(8,128)} %stem.1, bf16[2,3,768,768]{3,2,1,0:T(8,128)(2,1)} %weight.1, f32[2,768]{1,0:T(2,128)} %bias.1, bf16[768,768]{1,0:T(8,128)(2,1)} %query_weight.1, bf16[768,768]{1,0:T(8,128)(2,1)} %key_weight.1, bf16[768,768]{1,0:T(8,128)(2,1)} %value_weight.1, ...), custom_call_target="tpu_custom_call" | custom-call | flops 72477573120 | bytes 12582912 | tf_op jit(solution)/shard_map/tower/pallas_call | solution.py:420
  151.8 0.0 copy-start
  151.8 2.7 %copy.11 = f32[2048,768]{1,0:T(8,128)} copy(f32[2048,768]{1,0:T(8,128)S(1)} %get-tuple-element.2) | data formatting | bytes 12582912
  154.5 0.0 copy-done
  154.5 0.6 copy.12
Async XLA Ops:
  151.8 2.7 %copy-start = (f32[16,768]{1,0:T(8,128)S(1)}, f32[16,768]{1,0:T(8,128)}, u32[]{:S(2)}) copy-start(f32[16,768]{1,0:T(8,128)} %get-tuple-element.7) | copy-start | bytes 147460

commit v12 on v7

--- a/solution.py
+++ b/solution.py
@@ -18,6 +18,7 @@
 ORDER = (1, 2, 6, 5, 4, 3, 7)
 ROUND = (2, 4, 6)
 HEADS_AT_ONCE = 4
+WRITES = 16
 MESH = pl.DeviceIdType.MESH
 F32, BF16 = jnp.float32, jnp.bfloat16
 
@@ -424,6 +425,19 @@
     lax.fori_loop(0, CHUNKS, finish, 0)
 
 
+def write_kernel(tower, attended, tower_out, attended_out, sems):
+    size = tower.shape[0] // WRITES
+    copies = [
+        pltpu.make_async_copy(tower.at[pl.ds(k * size, size)], tower_out.at[pl.ds(k * size, size)], sems.at[k])
+        for k in range(WRITES)
+    ]
+    copies.append(pltpu.make_async_copy(attended, attended_out, sems.at[WRITES]))
+    for copy in copies:
+        copy.start()
+    for copy in copies:
+        copy.wait()
+
+
 def shards(stem_activity, convolution_weight, convolution_bias, query_weight, key_weight, value_weight, output_weight):
     length, chans = stem_activity.shape
     part = length // MEMBERS
@@ -432,11 +446,11 @@
     pooled = length // POOL
     dma, vmem = pltpu.SemaphoreType.DMA, pltpu.VMEM
     far, on_core = pl.BlockSpec(memory_space=pltpu.HBM), pl.BlockSpec(memory_space=vmem)
-    return pl.pallas_call(
+    results = pl.pallas_call(
         tower_kernel,
         out_shape=(
             vmem((length, chans), F32),
-            jax.ShapeDtypeStruct((pooled, chans), F32),
+            vmem((pooled, chans), F32),
         ),
         in_specs=[far, far, on_core, far, far, far, far],
         out_specs=(on_core, on_core),
@@ -475,6 +489,15 @@
         stem_activity, convolution_weight, convolution_bias,
         query_weight, key_weight, value_weight, output_weight,
     )
+    return pl.pallas_call(
+        write_kernel,
+        out_shape=[jax.ShapeDtypeStruct(result.shape, F32) for result in results],
+        in_specs=[on_core, on_core],
+        out_specs=[far, far],
+        scratch_shapes=[dma((WRITES + 1,))],
+        cost_estimate=pl.CostEstimate(flops=0, bytes_accessed=8 * length * chans, transcendentals=0),
+        name="write",
+    )(*results)
 
 
 def solution(mesh):

time: 155 us -> 160 us (1.032)
  Pallas kernels: 151 us -> 156 us
    pallas_call x1 -> x2, Pallas kernels: 151 us -> 156 us  [the longest x1 151 us: shards(): pl.pallas_call(tower_kernel, out_shape=(vmem((length, chans), F32), vmem(...]
where the time goes in v12:
time: 160 us
  Pallas kernels  156 us (98%)
  local copies, waits for them, and re-layouts  3.24 us (2%)
    pallas_call x1, Pallas kernels, shards(): pl.pallas_call(tower_kernel, out_shape=(vmem((length, chans), F32), vmem(...  151 us
    pallas_call x1, Pallas kernels, shards(): pl.pallas_call(write_kernel, out_shape=[jax.ShapeDtypeStruct(result.shape...  5.57 us
    unnamed x4, local copies, waits for them, and re-layouts  3.24 us

profile of v12, /device:TPU:4, one launch (start us, length us, event | category | flops | bytes accessed | tf_op | source)
XLA Modules:
  0.0 160.3 jit_solution(9418116230755154324)
XLA Ops:
  0.6 150.6 %tower.1 = (f32[2048,768]{1,0:T(8,128)S(1)}, f32[16,768]{1,0:T(8,128)S(1)}) custom-call(f32[2048,768]{1,0:T(8,128)} %stem.1, bf16[2,3,768,768]{3,2,1,0:T(8,128)(2,1)} %weight.1, f32[2,768]{1,0:T(2,128)} %bias.1, bf16[768,768]{1,0:T(8,128)(2,1)} %query_weight.1, bf16[768,768]{1,0:T(8,128)(2,1)} %key_weight.1, bf16[768,768]{1,0:T(8,128)(2,1)} %value_weight.1, ...), custom_call_target="tpu_custom_call" | custom-call | flops 72477573120 | bytes 12582912 | tf_op jit(solution)/shard_map/tower/pallas_call | solution.py:449
  151.3 0.0 copy-start
  151.3 2.6 %copy-done = f32[2048,768]{1,0:T(8,128)} copy-done((f32[2048,768]{1,0:T(8,128)}, f32[2048,768]{1,0:T(8,128)S(1)}, u32[]{:S(2)}) %copy-start) | copy-done | bytes 6291480
  153.9 0.0 copy-start.1
  153.9 0.6 copy-done.1
  154.5 5.6 %write.1 = (f32[2048,768]{1,0:T(8,128)}, f32[16,768]{1,0:T(8,128)}) custom-call(f32[2048,768]{1,0:T(8,128)} %copy-done, f32[16,768]{1,0:T(8,128)} %copy-done.1), custom_call_target="tpu_custom_call" | custom-call | bytes 12582912 | tf_op jit(solution)/shard_map/write/pallas_call | solution.py:492
Async XLA Ops:
  151.3 2.6 %copy-start = (f32[2048,768]{1,0:T(8,128)}, f32[2048,768]{1,0:T(8,128)S(1)}, u32[]{:S(2)}) copy-start(f32[2048,768]{1,0:T(8,128)S(1)} %get-tuple-element.4.tower) | copy-start | bytes 18874372
  153.9 0.6 copy-start.1

commit v13 on v7

--- a/solution.py
+++ b/solution.py
@@ -97,13 +97,6 @@
         return pltpu.make_async_copy(source, heads_weight.at[k], heads_sem.at[k])
 
     every_tap = [(layer, tap, half) for layer in range(2) for tap in range(3) for half in range(2)]
-    for side in range(2):
-        @pl.when(jnp.logical_not(has[side]))
-        def _():
-            rows_in[0 if side else HALO + MEMBERS : HALO if side else 2 * HALO + MEMBERS] = jnp.zeros(
-                (HALO, part, chans), F32
-            )
-
     pl.semaphore_wait(barrier, MEMBERS + has[0].astype(jnp.int32) + has[1].astype(jnp.int32))
 
     def span(chunk):
@@ -307,6 +300,13 @@
         start_in(chunk)
     for which in every_tap:
         load_taps(*which).start()
+    for side in range(2):
+        @pl.when(jnp.logical_not(has[side]))
+        def _():
+            rows_in[0 if side else HALO + MEMBERS : HALO if side else 2 * HALO + MEMBERS] = jnp.zeros(
+                (HALO, part, chans), F32
+            )
+
     for chunk in range(AHEAD):
         forward(chunk)
         start_in(chunk + IN_FLIGHT)

time: 155 us -> 155 us (level)
  no operation moved by 1% of the time
where the time goes in v13:
time: 155 us
  Pallas kernels  151 us (97%)
  local copies, waits for them, and re-layouts  3.33 us (2%)
    pallas_call x1, Pallas kernels, shards(): pl.pallas_call(tower_kernel, out_shape=(vmem((length, chans), F32), jax.S...  151 us
    unnamed x4, local copies, waits for them, and re-layouts  3.33 us

profile of v13, /device:TPU:4, one launch (start us, length us, event | category | flops | bytes accessed | tf_op | source)
XLA Modules:
  0.0 155.2 jit_solution(6741169222119346948)
XLA Ops:
  0.6 151.3 %tower.1 = (f32[2048,768]{1,0:T(8,128)S(1)}, f32[16,768]{1,0:T(8,128)}) custom-call(f32[2048,768]{1,0:T(8,128)} %stem.1, bf16[2,3,768,768]{3,2,1,0:T(8,128)(2,1)} %weight.1, f32[2,768]{1,0:T(2,128)} %bias.1, bf16[768,768]{1,0:T(8,128)(2,1)} %query_weight.1, bf16[768,768]{1,0:T(8,128)(2,1)} %key_weight.1, bf16[768,768]{1,0:T(8,128)(2,1)} %value_weight.1, ...), custom_call_target="tpu_custom_call" | custom-call | flops 72477573120 | bytes 12582912 | tf_op jit(solution)/shard_map/tower/pallas_call | solution.py:435
  151.9 0.0 copy-start
  151.9 2.7 %copy.11 = f32[2048,768]{1,0:T(8,128)} copy(f32[2048,768]{1,0:T(8,128)S(1)} %get-tuple-element.2) | data formatting | bytes 12582912
  154.6 0.0 copy-done
  154.6 0.6 copy.12
Async XLA Ops:
  151.9 2.7 %copy-start = (f32[16,768]{1,0:T(8,128)S(1)}, f32[16,768]{1,0:T(8,128)}, u32[]{:S(2)}) copy-start(f32[16,768]{1,0:T(8,128)} %get-tuple-element.7) | copy-start | bytes 147460

commit v14 on v13

--- a/solution.py
+++ b/solution.py
@@ -11,7 +11,7 @@
 MEMBERS = 8
 HALO = 3
 CHUNKS = 8
-IN_FLIGHT = 3
+IN_FLIGHT = 6
 HELD = 4
 AHEAD = 1
 COLUMNS = 256

time: 155 us -> 155 us (level)
  no operation moved by 1% of the time
where the time goes in v14:
time: 155 us
  Pallas kernels  151 us (97%)
  local copies, waits for them, and re-layouts  3.33 us (2%)
    pallas_call x1, Pallas kernels, shards(): pl.pallas_call(tower_kernel, out_shape=(vmem((length, chans), F32), jax.S...  151 us
    unnamed x4, local copies, waits for them, and re-layouts  3.33 us

profile of v14, /device:TPU:4, one launch (start us, length us, event | category | flops | bytes accessed | tf_op | source)
XLA Modules:
  0.0 155.2 jit_solution(5897532407662426945)
XLA Ops:
  0.6 151.3 %tower.1 = (f32[2048,768]{1,0:T(8,128)S(1)}, f32[16,768]{1,0:T(8,128)}) custom-call(f32[2048,768]{1,0:T(8,128)} %stem.1, bf16[2,3,768,768]{3,2,1,0:T(8,128)(2,1)} %weight.1, f32[2,768]{1,0:T(2,128)} %bias.1, bf16[768,768]{1,0:T(8,128)(2,1)} %query_weight.1, bf16[768,768]{1,0:T(8,128)(2,1)} %key_weight.1, bf16[768,768]{1,0:T(8,128)(2,1)} %value_weight.1, ...), custom_call_target="tpu_custom_call" | custom-call | flops 72477573120 | bytes 12582912 | tf_op jit(solution)/shard_map/tower/pallas_call | solution.py:435
  151.9 0.0 copy-start
  151.9 2.7 %copy.11 = f32[2048,768]{1,0:T(8,128)} copy(f32[2048,768]{1,0:T(8,128)S(1)} %get-tuple-element.2) | data formatting | bytes 12582912
  154.6 0.0 copy-done
  154.6 0.6 copy.12
Async XLA Ops:
  151.9 2.7 %copy-start = (f32[16,768]{1,0:T(8,128)S(1)}, f32[16,768]{1,0:T(8,128)}, u32[]{:S(2)}) copy-start(f32[16,768]{1,0:T(8,128)} %get-tuple-element.7) | copy-start | bytes 147460

commit v15 on v14

--- a/solution.py
+++ b/solution.py
@@ -12,7 +12,7 @@
 HALO = 3
 CHUNKS = 8
 IN_FLIGHT = 6
-HELD = 4
+HELD = 3
 AHEAD = 1
 COLUMNS = 256
 ORDER = (1, 2, 6, 5, 4, 3, 7)

time: 155 us -> 155 us (level)
  no operation moved by 1% of the time
where the time goes in v15:
time: 155 us
  Pallas kernels  151 us (97%)
  local copies, waits for them, and re-layouts  3.33 us (2%)
    pallas_call x1, Pallas kernels, shards(): pl.pallas_call(tower_kernel, out_shape=(vmem((length, chans), F32), jax.S...  151 us
    unnamed x4, local copies, waits for them, and re-layouts  3.33 us

profile of v15, /device:TPU:4, one launch (start us, length us, event | category | flops | bytes accessed | tf_op | source)
XLA Modules:
  0.0 155.1 jit_solution(12831664174397376936)
XLA Ops:
  0.6 151.1 %tower.1 = (f32[2048,768]{1,0:T(8,128)S(1)}, f32[16,768]{1,0:T(8,128)}) custom-call(f32[2048,768]{1,0:T(8,128)} %stem.1, bf16[2,3,768,768]{3,2,1,0:T(8,128)(2,1)} %weight.1, f32[2,768]{1,0:T(2,128)} %bias.1, bf16[768,768]{1,0:T(8,128)(2,1)} %query_weight.1, bf16[768,768]{1,0:T(8,128)(2,1)} %key_weight.1, bf16[768,768]{1,0:T(8,128)(2,1)} %value_weight.1, ...), custom_call_target="tpu_custom_call" | custom-call | flops 72477573120 | bytes 12582912 | tf_op jit(solution)/shard_map/tower/pallas_call | solution.py:435
  151.8 0.0 copy-start
  151.8 2.7 %copy.11 = f32[2048,768]{1,0:T(8,128)} copy(f32[2048,768]{1,0:T(8,128)S(1)} %get-tuple-element.2) | data formatting | bytes 12582912
  154.5 0.0 copy-done
  154.5 0.6 copy.12
Async XLA Ops:
  151.8 2.7 %copy-start = (f32[16,768]{1,0:T(8,128)S(1)}, f32[16,768]{1,0:T(8,128)}, u32[]{:S(2)}) copy-start(f32[16,768]{1,0:T(8,128)} %get-tuple-element.7) | copy-start | bytes 147460
